TPU v7x, 32 devices: a whole 2x2x4 slice. The times are simulated.
32 devices in a mesh: grp: 2 (over x), col: 16 (over z, y, core).
Axes of the slice: x: 2, y: 2, z: 4, core: 2. Of those that a mesh axis runs over, the one named last changes fastest.
Arguments:
- base_velocity: float32 [81, 4096], P(None, ('grp', 'col')), parts along dimension 1, may hold values from -6 to 6
- viscosity: float32 [4096], P(('grp', 'col')), parts along dimension 0, may hold values from 1 to 2
- friction: float32 [9, 4096], P(None, ('grp', 'col')), parts along dimension 1, may hold values from 0.5 to 4
- obs_weight: float32 [9, 4096], P(None, ('grp', 'col')), parts along dimension 1, may hold values from 20 to 80
- stiffness: float32 [81, 81], replicated, may hold values from -0.025 to 6, as said below
- face_coupling: float32 [27, 27], replicated, may hold values from 0 to 0.022222222, as said below
- face_rows: int32 [4, 27], replicated, may hold values from 0 to 80, as said below
- tile_source: int32 [16, 128], P('col'), may hold values from 0 to 127, each once within a row
- probes: float32 [9, 16, 4096], P(None, None, ('grp', 'col')), parts along dimension 2, may hold values from -6 to 6
Outputs:
- hessian_action: float32 [9, 16, 4096], P(None, None, ('grp', 'col')), parts along dimension 2
- adjoint_state: float32 [81, 16, 4096], P(None, None, ('grp', 'col')), parts along dimension 2
There are 2 independent parts, one for each index of `grp`. A program takes and returns all parts, laid end to end along the dimension named above; an argument that names none is the same for every part. Nothing has to cross between parts.
Inputs may be any that keep to these rules, and one draw needn't show every extreme that they name: `stiffness`: symmetric. `face_coupling`: nonnegative. `face_rows`: 27 distinct numbers in each row. `tile_source`: each row holds every number below 128 once.
All inputs are finite; a program needn't handle non-finite values.
Results may differ from a plain program's by a relative error of at most 0.0003.
Values sent between devices are 32-bit elements; how exact they have to be, the bound alone decides.
A program may use at most 64 MiB of HBM per device.

v0:
```python
import jax
import jax.numpy as jnp
from jax import lax
from jax.sharding import PartitionSpec as P

DOF = 81
BASAL = 9
ITERS = 2
TB = 32


def from_behind(value, axis, by):
    size = lax.axis_size(axis)
    pairs = [(i, i + by) for i in range(size) if 0 <= i + by < size]
    return lax.ppermute(value, axis, pairs)


def couple_local(field, face_coupling, face_rows):
    count = lax.axis_size("col")
    levels = count.bit_length() - 1
    across = 1 << levels // 2
    along = count // across
    position = lax.axis_index("col")
    row_place = position % along
    depth, width = (field.shape[0], field.shape[1])
    grid = field.reshape(depth, width, field.shape[2] // TB, TB)
    west, east, south, north = (face_rows[0], face_rows[1], face_rows[2], face_rows[3])
    high_edge = grid[:, :, -1]
    low_edge = grid[:, :, 0]
    top_edge = grid[:, :, :, -1]
    bottom_edge = grid[:, :, :, 0]
    from_west = from_behind(high_edge, "col", along)
    from_east = from_behind(low_edge, "col", -along)
    from_south = from_behind(top_edge, "col", 1)
    from_north = from_behind(bottom_edge, "col", -1)
    from_south = jnp.where(row_place > 0, from_south, 0.0)
    from_north = jnp.where(row_place < along - 1, from_north, 0.0)
    from_west = jnp.take(from_west, east, axis=0)
    from_east = jnp.take(from_east, west, axis=0)
    from_south = jnp.take(from_south, north, axis=0)
    from_north = jnp.take(from_north, south, axis=0)
    west_vals = jnp.take(grid, west, axis=0)
    east_vals = jnp.take(grid, east, axis=0)
    south_vals = jnp.take(grid, south, axis=0)
    north_vals = jnp.take(grid, north, axis=0)
    west_next = jnp.concatenate([west_vals[:, :, 1:], from_east[:, :, None]], axis=2)
    east_prev = jnp.concatenate([from_west[:, :, None], east_vals[:, :, :-1]], axis=2)
    south_next = jnp.concatenate([south_vals[:, :, :, 1:], from_north[:, :, :, None]], axis=3)
    north_prev = jnp.concatenate([from_south[:, :, :, None], north_vals[:, :, :, :-1]], axis=3)
    to_east = jnp.einsum("fg,gqab->fqab", face_coupling, west_next, precision=lax.Precision.HIGHEST)
    to_west = jnp.einsum("gf,gqab->fqab", face_coupling, east_prev, precision=lax.Precision.HIGHEST)
    to_north = jnp.einsum(
        "fg,gqab->fqab", face_coupling, south_next, precision=lax.Precision.HIGHEST
    )
    to_south = jnp.einsum(
        "gf,gqab->fqab", face_coupling, north_prev, precision=lax.Precision.HIGHEST
    )
    total = jnp.zeros_like(grid)
    total = total.at[east].add(-to_east)
    total = total.at[west].add(-to_west)
    total = total.at[north].add(-to_north)
    total = total.at[south].add(-to_south)
    return total.reshape(field.shape)


def apply_field(field, viscosity, friction, stiffness, face_coupling, face_rows):
    inner = jnp.einsum("kj,jqt->kqt", stiffness, field, precision=lax.Precision.HIGHEST)
    basal = jnp.pad(friction[:, None, :] * field[:BASAL], ((0, DOF - BASAL), (0, 0), (0, 0)))
    return viscosity[None, None, :] * inner + basal + couple_local(field, face_coupling, face_rows)


def local_sum(left, right):
    return jnp.sum(left * right, axis=(0, 2))


def square_total(resid):
    return lax.psum(local_sum(resid, resid), "col")[None, :, None]


def curve_total(direction, image):
    return lax.psum(local_sum(direction, image), "col")[None, :, None]


def solve(rhs, operate):
    solution = jnp.zeros_like(rhs)
    resid = rhs
    direction = rhs
    norm_now = square_total(resid)
    for step in range(ITERS):
        image = operate(direction)
        alpha = norm_now / curve_total(direction, image)
        solution = solution + alpha * direction
        resid = resid - alpha * image
        if step + 1 < ITERS:
            norm_next = square_total(resid)
            direction = resid + norm_next / norm_now * direction
            norm_now = norm_next
    return solution


def local(
    base_velocity,
    viscosity,
    friction,
    obs_weight,
    stiffness,
    face_coupling,
    face_rows,
    tile_source,
    probes,
):
    order = tile_source[0]
    received = lax.all_to_all(probes, "col", split_axis=2, concat_axis=2, tiled=True)
    tile_probe = jnp.take(received, order, axis=2)
    basal_scale = friction * base_velocity[:BASAL]

    def operate(field):
        return apply_field(field, viscosity, friction, stiffness, face_coupling, face_rows)

    force = -jnp.pad(basal_scale[:, None, :] * tile_probe, ((0, DOF - BASAL), (0, 0), (0, 0)))
    forward = solve(force, operate)
    misfit = -jnp.pad(
        obs_weight[:, None, :] * forward[DOF - BASAL :], ((DOF - BASAL, 0), (0, 0), (0, 0))
    )
    adjoint_state = solve(misfit, operate)
    tile_action = basal_scale[:, None, :] * adjoint_state[:BASAL]
    placed = jnp.zeros_like(tile_action).at[:, :, order].set(tile_action)
    hessian_action = lax.all_to_all(placed, "col", split_axis=2, concat_axis=2, tiled=True)
    return (hessian_action, adjoint_state)


def solution(mesh):
    placed = (
        P(None, ("grp", "col")),
        P(("grp", "col")),
        P(None, ("grp", "col")),
        P(None, ("grp", "col")),
        P(),
        P(),
        P(),
        P("col", None),
        P(None, None, ("grp", "col")),
    )
    return jax.shard_map(
        local,
        mesh=mesh,
        in_specs=placed,
        out_specs=(P(None, None, ("grp", "col")), P(None, None, ("grp", "col"))),
        check_vma=False,
    )
```

profile of v0, /device:TPU:0, one launch (start us, length us, event | category | flops | bytes accessed | tf_op | source)
XLA Modules:
  0.0 557.0 jit_solution(12097981674849629166)
XLA Ops:
  2.9 7.4 %all-to-all-start = ((f32[16,1,1152]{2,1,0:T(1,128)}), f32[16,1,1152]{2,1,0:T(1,128)S(1)}, u32[]{:S(2)}, u32[]{:S(2)}) async-start(f32[16,1,1152]{2,1,0:T(1,128)} %reshape.711), calls=%async_computation | async-start | bytes 147456 | tf_op jit(solution)/shard_map/all_to_all | solution.py:113
  38.7 5.2 collective-permute-start.1
  53.6 4.2 collective-permute-start.3
  83.1 3.9 scatter_fusion
  87.0 3.7 scatter_fusion.1
  90.8 3.7 scatter_fusion.2
  94.5 3.7 scatter_fusion.3
  103.3 29.9 %all-reduce.7 = (f32[16]{0:T(128)S(1)}, f32[16]{0:T(128)S(1)}) all-reduce(f32[16]{0:T(128)S(1)} %get-tuple-element.14, f32[16]{0:T(128)S(1)} %get-tuple-element.13), channel_id=1, replica_groups=mesh['grp'=2,'col'=16] {'col'}, use_global_device_ids=true, to_apply=%region_1.2 | all-reduce | flops 32 | bytes 256 | tf_op jit(solution)/shard_map/psum | solution.py:77
  133.5 29.5 %psum.58 = f32[16]{0:T(128)S(1)} all-reduce(f32[16]{0:T(128)S(1)} %multiply_reduce_fusion.1), channel_id=1, replica_groups=mesh['grp'=2,'col'=16] {'col'}, use_global_device_ids=true, to_apply=%region_9.13 | all-reduce | flops 16 | bytes 128 | tf_op jit(solution)/shard_map/psum | solution.py:77
  229.1 4.1 scatter_fusion.4
  233.2 3.8 scatter_fusion.5
  237.1 3.8 scatter_fusion.6
  240.9 3.8 scatter_fusion.7
  250.7 32.9 %psum.59 = f32[16]{0:T(128)S(1)} all-reduce(f32[16]{0:T(128)S(1)} %fusion.31), channel_id=1, replica_groups=mesh['grp'=2,'col'=16] {'col'}, use_global_device_ids=true, to_apply=%region_15.19 | all-reduce | flops 16 | bytes 128 | tf_op jit(solution)/shard_map/psum | solution.py:81
  342.0 3.9 scatter_fusion.8
  345.9 3.7 scatter_fusion.9
  349.6 3.7 scatter_fusion.10
  362.2 34.0 %all-reduce.6 = (f32[16]{0:T(128)S(1)}, f32[16]{0:T(128)S(1)}) all-reduce(f32[16]{0:T(128)S(1)} %get-tuple-element.12, f32[16]{0:T(128)S(1)} %get-tuple-element.11), channel_id=1, replica_groups=mesh['grp'=2,'col'=16] {'col'}, use_global_device_ids=true, to_apply=%region_17.21 | all-reduce | flops 32 | bytes 256 | tf_op jit(solution)/shard_map/psum | solution.py:77
  396.5 29.5 %psum.62 = f32[16]{0:T(128)S(1)} all-reduce(f32[16]{0:T(128)S(1)} %multiply_reduce_fusion), channel_id=1, replica_groups=mesh['grp'=2,'col'=16] {'col'}, use_global_device_ids=true, to_apply=%region_25.29 | all-reduce | flops 16 | bytes 128 | tf_op jit(solution)/shard_map/psum | solution.py:77
  456.2 5.5 collective-permute-start.13
  486.8 4.0 scatter_fusion.12
  507.9 30.3 %psum.63 = f32[16]{0:T(128)S(1)} all-reduce(f32[16]{0:T(128)S(1)} %fusion.30), channel_id=1, replica_groups=mesh['grp'=2,'col'=16] {'col'}, use_global_device_ids=true, to_apply=%region_31.35 | all-reduce | flops 16 | bytes 128 | tf_op jit(solution)/shard_map/psum | solution.py:81
  539.0 4.3 scatter_fusion.16
  548.7 6.0 %all-to-all-done.1 = f32[16,1,1152]{2,1,0:T(1,128)S(1)} async-done(((f32[16,1,1152]{2,1,0:T(1,128)}), f32[16,1,1152]{2,1,0:T(1,128)S(1)}, u32[]{:S(2)}, u32[]{:S(2)}) %all-to-all-start.1) | async-done | bytes 73760 | tf_op jit(solution)/shard_map/all_to_all | solution.py:128
  (400 shorter events, 289.9 us)
Async XLA Ops:
  0.6 101.7 %copy-start = (f32[81,81]{1,0:T(8,128)S(1)}, f32[81,81]{1,0:T(8,128)}, u32[]{:S(2)}) copy-start(f32[81,81]{1,0:T(8,128)} %param.19) | copy-start | bytes 78736
  2.9 14.4 %all-to-all-start = ((f32[16,1,1152]{2,1,0:T(1,128)}), f32[16,1,1152]{2,1,0:T(1,128)S(1)}, u32[]{:S(2)}, u32[]{:S(2)}) async-start(f32[16,1,1152]{2,1,0:T(1,128)} %reshape.711), calls=%async_computation | async-start | bytes 147456 | tf_op jit(solution)/shard_map/all_to_all | solution.py:113
  12.5 54.2 %copy-start.35 = (pred[27]{0:T(512)(128)(4,1)}, pred[27]{0:T(512)(128)(4,1)S(1)}, u32[]{:S(2)}) copy-start(pred[27]{0:T(512)(128)(4,1)S(1)} %get-tuple-element.47) | copy-start | bytes 85
  12.5 57.8 %copy-start.32 = (pred[27]{0:T(512)(128)(4,1)}, pred[27]{0:T(512)(128)(4,1)S(1)}, u32[]{:S(2)}) copy-start(pred[27]{0:T(512)(128)(4,1)S(1)} %get-tuple-element.19) | copy-start | bytes 85
  12.5 62.7 %copy-start.29 = (pred[27]{0:T(512)(128)(4,1)}, pred[27]{0:T(512)(128)(4,1)S(1)}, u32[]{:S(2)}) copy-start(pred[27]{0:T(512)(128)(4,1)S(1)} %get-tuple-element.45) | copy-start | bytes 85
  33.4 39.6 %collective-permute-start = (f32[81,16,32]{0,2,1:T(8,128)}, f32[81,16,32]{0,2,1:T(8,128)}, u32[]{:S(2)}, u32[]{:S(2)}) collective-permute-start(f32[81,16,32]{0,2,1:T(8,128)} %get-tuple-element.42), channel_id=1, source_target_pairs={{4,0},{5,1},{6,2},{7,3},{8,4},{9,5},{10,6},{11,7},{12,8},{13,9},{1... | collective-permute-start | bytes 497672 | tf_op jit(solution)/shard_map/ppermute | solution.py:15
  38.7 39.2 %collective-permute-start.1 = (f32[81,16,32]{0,2,1:T(8,128)}, f32[81,16,32]{0,2,1:T(8,128)}, u32[]{:S(2)}, u32[]{:S(2)}) collective-permute-start(f32[81,16,32]{0,2,1:T(8,128)} %get-tuple-element.41), channel_id=1, source_target_pairs={{0,4},{1,5},{2,6},{3,7},{4,8},{5,9},{6,10},{7,11},{8,12},{9,13},{1... | collective-permute-start | bytes 497672 | tf_op jit(solution)/shard_map/ppermute | solution.py:15
  45.4 19.5 %collective-permute-start.2 = (f32[81,16,4]{1,2,0:T(4,128)}, f32[81,16,4]{1,2,0:T(4,128)}, u32[]{:S(2)}, u32[]{:S(2)}) collective-permute-start(f32[81,16,4]{1,2,0:T(4,128)} %bitcast.25), channel_id=1, source_target_pairs={{1,0},{2,1},{3,2},{4,3},{5,4},{6,5},{7,6},{8,7},{9,8},{10,9},{11,1... | collective-permute-start | bytes 62216 | tf_op jit(solution)/shard_map/ppermute | solution.py:15
  53.6 15.7 %collective-permute-start.3 = (f32[81,16,4]{1,2,0:T(4,128)S(1)}, f32[81,16,4]{1,2,0:T(4,128)}, u32[]{:S(2)}, u32[]{:S(2)}) collective-permute-start(f32[81,16,4]{1,2,0:T(4,128)S(1)} %bitcast.242), channel_id=1, source_target_pairs={{0,1},{1,2},{2,3},{3,4},{4,5},{5,6},{6,7},{7,8},{8,9},{9,10},{10,1... | collective-permute-start | bytes 62216 | tf_op jit(solution)/shard_map/ppermute | solution.py:15
  183.0 25.7 %collective-permute-start.7 = (f32[81,16,4]{1,2,0:T(4,128)S(1)}, f32[81,16,4]{1,2,0:T(4,128)}, u32[]{:S(2)}, u32[]{:S(2)}) collective-permute-start(f32[81,16,4]{1,2,0:T(4,128)S(1)} %bitcast.240), channel_id=1, source_target_pairs={{0,1},{1,2},{2,3},{3,4},{4,5},{5,6},{6,7},{7,8},{8,9},{9,10},{10,1... | collective-permute-start | bytes 62216 | tf_op jit(solution)/shard_map/ppermute | solution.py:15
  190.9 23.6 %collective-permute-start.6 = (f32[81,16,4]{1,2,0:T(4,128)}, f32[81,16,4]{1,2,0:T(4,128)}, u32[]{:S(2)}, u32[]{:S(2)}) collective-permute-start(f32[81,16,4]{1,2,0:T(4,128)} %bitcast.43), channel_id=1, source_target_pairs={{1,0},{2,1},{3,2},{4,3},{5,4},{6,5},{7,6},{8,7},{9,8},{10,9},{11,1... | collective-permute-start | bytes 62216 | tf_op jit(solution)/shard_map/ppermute | solution.py:15
  198.7 20.3 %collective-permute-start.5 = (f32[81,16,32]{0,2,1:T(8,128)S(1)}, f32[81,16,32]{0,2,1:T(8,128)}, u32[]{:S(2)}, u32[]{:S(2)}) collective-permute-start(f32[81,16,32]{0,2,1:T(8,128)S(1)} %copy-done.19), channel_id=1, source_target_pairs={{0,4},{1,5},{2,6},{3,7},{4,8},{5,9},{6,10},{7,11},{8,12},{9,13},{1... | collective-permute-start | bytes 497672 | tf_op jit(solution)/shard_map/ppermute | solution.py:15
  207.2 16.8 %collective-permute-start.4 = (f32[81,16,32]{0,2,1:T(8,128)}, f32[81,16,32]{0,2,1:T(8,128)}, u32[]{:S(2)}, u32[]{:S(2)}) collective-permute-start(f32[81,16,32]{0,2,1:T(8,128)} %get-tuple-element.38), channel_id=1, source_target_pairs={{4,0},{5,1},{6,2},{7,3},{8,4},{9,5},{10,6},{11,7},{12,8},{13,9},{1... | collective-permute-start | bytes 497672 | tf_op jit(solution)/shard_map/ppermute | solution.py:15
  247.3 36.4 %copy-start.54 = (f32[16]{0:T(128)S(1)}, f32[16]{0:T(128)}, u32[]{:S(2)}) copy-start(f32[16]{0:T(128)} %copy-done.53) | copy-start | bytes 196
  283.8 142.2 %copy-start.1 = (f32[9,16,128]{2,0,1:T(8,128)}, f32[9,16,128]{2,0,1:T(8,128)S(1)}, u32[]{:S(2)}) copy-start(f32[9,16,128]{2,0,1:T(8,128)S(1)} %fusion.101) | copy-start | bytes 221188
  301.0 21.7 %collective-permute-start.11 = (f32[81,16,4]{1,2,0:T(4,128)S(1)}, f32[81,16,4]{1,2,0:T(4,128)}, u32[]{:S(2)}, u32[]{:S(2)}) collective-permute-start(f32[81,16,4]{1,2,0:T(4,128)S(1)} %bitcast.241), channel_id=1, source_target_pairs={{0,1},{1,2},{2,3},{3,4},{4,5},{5,6},{6,7},{7,8},{8,9},{9,10},{10,1... | collective-permute-start | bytes 62216 | tf_op jit(solution)/shard_map/ppermute | solution.py:15
  308.3 20.2 %collective-permute-start.10 = (f32[81,16,4]{1,2,0:T(4,128)}, f32[81,16,4]{1,2,0:T(4,128)}, u32[]{:S(2)}, u32[]{:S(2)}) collective-permute-start(f32[81,16,4]{1,2,0:T(4,128)} %bitcast.58), channel_id=1, source_target_pairs={{1,0},{2,1},{3,2},{4,3},{5,4},{6,5},{7,6},{8,7},{9,8},{10,9},{11,1... | collective-permute-start | bytes 62216 | tf_op jit(solution)/shard_map/ppermute | solution.py:15
  313.0 19.9 %collective-permute-start.9 = (f32[81,16,32]{0,2,1:T(8,128)S(1)}, f32[81,16,32]{0,2,1:T(8,128)S(1)}, u32[]{:S(2)}, u32[]{:S(2)}) collective-permute-start(f32[81,16,32]{0,2,1:T(8,128)S(1)} %copy-done.20), channel_id=1, source_target_pairs={{0,4},{1,5},{2,6},{3,7},{4,8},{5,9},{6,10},{7,11},{8,12},{9,13},{1... | collective-permute-start | bytes 497672 | tf_op jit(solution)/shard_map/ppermute | solution.py:15
  320.9 15.9 %collective-permute-start.8 = (f32[81,16,32]{0,2,1:T(8,128)}, f32[81,16,32]{0,2,1:T(8,128)}, u32[]{:S(2)}, u32[]{:S(2)}) collective-permute-start(f32[81,16,32]{0,2,1:T(8,128)} %get-tuple-element.34), channel_id=1, source_target_pairs={{4,0},{5,1},{6,2},{7,3},{8,4},{9,5},{10,6},{11,7},{12,8},{13,9},{1... | collective-permute-start | bytes 497672 | tf_op jit(solution)/shard_map/ppermute | solution.py:15
  447.0 17.8 %collective-permute-start.14 = (f32[81,16,4]{1,2,0:T(4,128)}, f32[81,16,4]{1,2,0:T(4,128)}, u32[]{:S(2)}, u32[]{:S(2)}) collective-permute-start(f32[81,16,4]{1,2,0:T(4,128)} %bitcast.73), channel_id=1, source_target_pairs={{1,0},{2,1},{3,2},{4,3},{5,4},{6,5},{7,6},{8,7},{9,8},{10,9},{11,1... | collective-permute-start | bytes 62216 | tf_op jit(solution)/shard_map/ppermute | solution.py:15
  448.4 18.2 %collective-permute-start.15 = (f32[81,16,4]{1,2,0:T(4,128)S(1)}, f32[81,16,4]{1,2,0:T(4,128)}, u32[]{:S(2)}, u32[]{:S(2)}) collective-permute-start(f32[81,16,4]{1,2,0:T(4,128)S(1)} %copy.227), channel_id=1, source_target_pairs={{0,1},{1,2},{2,3},{3,4},{4,5},{5,6},{6,7},{7,8},{8,9},{9,10},{10,1... | collective-permute-start | bytes 62216 | tf_op jit(solution)/shard_map/ppermute | solution.py:15
  454.8 20.4 %collective-permute-start.12 = (f32[81,16,32]{0,2,1:T(8,128)}, f32[81,16,32]{0,2,1:T(8,128)}, u32[]{:S(2)}, u32[]{:S(2)}) collective-permute-start(f32[81,16,32]{0,2,1:T(8,128)} %get-tuple-element.30), channel_id=1, source_target_pairs={{4,0},{5,1},{6,2},{7,3},{8,4},{9,5},{10,6},{11,7},{12,8},{13,9},{1... | collective-permute-start | bytes 497672 | tf_op jit(solution)/shard_map/ppermute | solution.py:15
  456.2 21.2 %collective-permute-start.13 = (f32[81,16,32]{0,2,1:T(8,128)}, f32[81,16,32]{0,2,1:T(8,128)}, u32[]{:S(2)}, u32[]{:S(2)}) collective-permute-start(f32[81,16,32]{0,2,1:T(8,128)} %get-tuple-element.29), channel_id=1, source_target_pairs={{0,4},{1,5},{2,6},{3,7},{4,8},{5,9},{6,10},{7,11},{8,12},{9,13},{1... | collective-permute-start | bytes 497672 | tf_op jit(solution)/shard_map/ppermute | solution.py:15
  544.2 10.5 %all-to-all-start.1 = ((f32[16,1,1152]{2,1,0:T(1,128)}), f32[16,1,1152]{2,1,0:T(1,128)S(1)}, u32[]{:S(2)}, u32[]{:S(2)}) async-start(f32[16,1,1152]{2,1,0:T(1,128)} %reshape.713), calls=%async_computation.1 | async-start | bytes 147456 | tf_op jit(solution)/shard_map/all_to_all | solution.py:128
  (60 other events, 650.8 us)
where the time goes:
time: 566 us; the launch traced here: 557 us
  local copies, waits for them, and re-layouts  191 us (34%)
  blocking collectives  186 us (33%)
  other arithmetic  95.6 us (17%)
  starting transfers between devices  48.6 us (9%)
  matrix products  25.3 us (4%)
  waiting for transfers between devices  8.03 us (1%)
    psum x4, blocking collectives, square_total(): return lax.psum(local_sum(resid, resid), 'col')[None, :, None]  123 us
    psum x2, blocking collectives, curve_total(): return lax.psum(local_sum(direction, image), 'col')[None, :, None]  63.2 us
    unnamed x156, local copies, waits for them, and re-layouts  39.7 us
    ppermute x16, starting transfers between devices, from_behind(): return lax.ppermute(value, axis, pairs)  37.7 us
    scatter-add x4, other arithmetic, couple_local(): total = total.at[east].add(-to_east)  15.9 us
    scatter-add x4, other arithmetic, couple_local(): total = total.at[west].add(-to_west)  15 us
    scatter-add x4, other arithmetic, couple_local(): total = total.at[north].add(-to_north)  15 us
    scatter-add x4, other arithmetic, couple_local(): total = total.at[south].add(-to_south)  15 us
  transfers between devices with their start and end apart: 18, of which 2 were waited for; matrix products, arithmetic and copies ran while one was open for 21% of the time, Pallas kernels for 0%

commit v1 on v0

v1 whole, which is shorter than its diff:
```python
import functools

import jax
import jax.numpy as jnp
from jax import lax
from jax.experimental import pallas as pl
from jax.experimental.pallas import tpu as pltpu
from jax.sharding import PartitionSpec as P

DOF = 81
BASAL = 9
TB = 32
LANES = 128
TOP = 72
ROWS = 96
BLOCK = 16
FACES = 32
F32 = jnp.float32
BF16 = jnp.bfloat16
MESH = pl.DeviceIdType.MESH


def dot_exact(a, b, dims=((1,), (0,))):
    return lax.dot_general(
        a, b, (dims, ((), ())), precision=lax.Precision.HIGHEST, preferred_element_type=F32
    )


def split(x):
    high = x.astype(BF16)
    return high, (x - high.astype(F32)).astype(BF16)


def dot(a, b):
    return jnp.dot(a, b, preferred_element_type=F32)


def iota(shape, axis):
    return lax.broadcasted_iota(jnp.int32, shape, axis)


def lane_of(rows):
    return iota((rows, LANES), 1)


def span(q):
    return slice(q * LANES, (q + 1) * LANES)


def roll(x, by):
    by = by % LANES
    return x if by == 0 else pltpu.roll(x, by, 1)


def pack_x(read, rows, a, probes):
    lane = lane_of(rows)
    out = []
    for k in range(probes // 4):
        block = jnp.zeros((rows, LANES), F32)
        for j in range(4):
            block = jnp.where(lane // TB == j, roll(read(4 * k + j), TB * (j - a)), block)
        out.append(block)
    return jnp.concatenate(out, axis=1)


def unpack_x(ref, q, a):
    return roll(ref[:, span(q // 4)], TB * (a - q % 4))


def pack_y(read, rows, b, probes):
    lane = lane_of(rows)
    block = jnp.zeros((rows, LANES), F32)
    for q in range(probes):
        block = jnp.where(lane % TB == q, roll(read(q), q - b), block)
    return block


def unpack_y(ref, q, b):
    return roll(ref[...], b - q)


def kernel(
    count,
    probes,
    vel_ref,
    visc_ref,
    fric_ref,
    obs_ref,
    stiff_ref,
    coup_ref,
    faces_ref,
    source_ref,
    probes_ref,
    hess_ref,
    adj_ref,
    pad_ref,
    fpad_ref,
    scale_ref,
    fric16_ref,
    obs16_ref,
    lf_h,
    lf_l,
    lg_h,
    lg_l,
    s_h,
    s_l,
    f_ref,
    g_ref,
    u_ref,
    w_ref,
    gf_ref,
    gg_ref,
    x_h,
    x_l,
    r_h,
    r_l,
    sr_ref,
    act_ref,
    red_ref,
    send1,
    recv1,
    send2,
    recv2,
    ar_ref,
    fx_out,
    fy_out,
    fx_in,
    fy_in,
    gx_out,
    gy_out,
    gx_in,
    gy_in,
    cx_out,
    cy_out,
    cx_in,
    cy_in,
    a2a_send,
    a2a_recv,
    ar_send,
    ar_recv,
    halo_send,
    halo_recv,
    edge_send,
    edge_recv,
):
    me = lax.axis_index("col")
    levels = count.bit_length() - 1
    across = 1 << (levels // 2)
    along = count // across
    gx = me // along
    gy = me % along
    has = (gx < across - 1, gx > 0, gy < along - 1, gy > 0)
    peer = (me + along, me - along, me + 1, me - 1)
    back = (1, 0, 3, 2)

    barrier = pltpu.get_barrier_semaphore()

    def greet(o, carry):
        pl.semaphore_signal(
            barrier, inc=1, device_id={"col": lax.rem(me + o, count)}, device_id_type=MESH
        )
        return carry

    lax.fori_loop(1, count, greet, 0)

    for buf in (fx_in, fy_in, gx_in, gy_in, cx_in, cy_in):
        buf[...] = jnp.zeros_like(buf)
    rows = []
    pad_ref[...] = jnp.zeros_like(pad_ref)
    for q in range(probes):
        pad_ref[0:BASAL, :] = probes_ref[:, q, :]
        rows.append(pad_ref[0:BLOCK, :])
    laid = jnp.concatenate(rows, axis=0)
    width = probes * BLOCK
    share = send1.shape[1]
    send1[...] = laid.T.reshape(count, share, width)
    recv1[pl.ds(me, 1)] = send1[pl.ds(me, 1)]

    pl.semaphore_wait(barrier, count - 1)

    def exchange(src, dst, send_sem, recv_sem, own):
        def one(o):
            other = lax.rem(me + o, count)
            return pltpu.make_async_remote_copy(
                src_ref=src.at[me if own else other],
                dst_ref=dst.at[me],
                send_sem=send_sem.at[other],
                recv_sem=recv_sem.at[me],
                device_id={"col": other},
                device_id_type=MESH,
            )

        def arrival(o):
            other = lax.rem(me + o, count)
            return pltpu.make_async_remote_copy(
                src_ref=src.at[me if own else other],
                dst_ref=dst.at[other],
                send_sem=send_sem.at[other],
                recv_sem=recv_sem.at[other],
                device_id={"col": other},
                device_id_type=MESH,
            )

        def loop(act):
            def body(o, carry):
                act(o)
                return carry

            lax.fori_loop(1, count, body, 0)

        start = lambda: loop(lambda o: one(o).start())
        receive = lambda: loop(lambda o: arrival(o).wait_recv())
        finish = lambda: loop(lambda o: one(o).wait_send())
        return start, receive, finish

    out_start, out_receive, out_finish = exchange(
        send1, recv1, a2a_send.at[0], a2a_recv.at[0], False
    )
    out_start()

    def padded(ref, height, width_):
        pad_ref[...] = jnp.zeros_like(pad_ref)
        pad_ref[0:height, 0:width_] = ref[...]
        return pad_ref[...]

    stiff = padded(stiff_ref, DOF, DOF)
    coup = padded(coup_ref, coup_ref.shape[0], coup_ref.shape[1])
    fpad_ref[...] = jnp.full_like(fpad_ref, -1)
    fpad_ref[0:4, 0 : faces_ref.shape[1]] = faces_ref[...]
    square = (LANES, LANES)
    hot = [
        jnp.where(iota(square, 0) == fpad_ref[k : k + 1, :], 1.0, 0.0).astype(F32)
        for k in range(4)
    ]
    pick = [h.T for h in hot]
    west, east, south, north = 0, 1, 2, 3
    cw = dot_exact(coup, pick[west])
    cs = dot_exact(coup, pick[south])
    m_e = dot_exact(hot[east], cw)
    m_n = dot_exact(hot[north], cs)
    m_w, m_s = m_e.T, m_n.T
    lane = lane_of(LANES)

    def columns(mats, first):
        out = jnp.zeros(square, F32)
        for i, m in enumerate(mats):
            if m is not None:
                out = jnp.where(lane // BLOCK == i, roll(m, BLOCK * i - first), out)
        return out

    operator = (stiff, -m_e, -m_w, -m_n, -m_s)
    lf = columns(operator, 0)
    lf_h[...], lf_l[...] = split(
        jnp.concatenate(
            [
                lf[:ROWS],
                columns((None, cw), 0)[:FACES],
                columns((None, None, None, cs), 0)[:FACES],
            ],
            axis=0,
        )
    )
    lg = columns(operator, TOP)
    lg_h[...], lg_l[...] = split(
        jnp.concatenate(
            [
                lg[:ROWS],
                columns((None, cw), TOP)[:FACES],
                columns((None, None, None, cs), TOP)[:FACES],
                dot_exact(cw, lg)[:FACES],
                dot_exact(cs, lg)[:FACES],
            ],
            axis=0,
        )
    )
    s_h[...], s_l[...] = split(
        jnp.concatenate(
            [stiff[:ROWS], cw[:FACES], cs[:FACES], pick[east][:FACES], pick[north][:FACES]], axis=0
        )
    )
    scale_ref[...] = jnp.zeros_like(scale_ref)
    scale_ref[0:BASAL, :] = fric_ref[...] * vel_ref[0:BASAL, :]
    fric16_ref[...] = jnp.zeros_like(fric16_ref)
    fric16_ref[0:BASAL, :] = fric_ref[...]
    obs16_ref[...] = jnp.zeros_like(obs16_ref)
    obs16_ref[0:BASAL, :] = obs_ref[...]
    order = jnp.where(iota(square, 0) == source_ref[...], 1.0, 0.0).astype(F32)
    visc = visc_ref[...]
    scale = scale_ref[...]
    fric16 = fric16_ref[...]
    obs16 = obs16_ref[...]

    def halo_copy(src, dst, d, sems, which):
        return pltpu.make_async_remote_copy(
            src_ref=src,
            dst_ref=dst,
            send_sem=sems[0].at[which],
            recv_sem=sems[1].at[which],
            device_id={"col": peer[d]},
            device_id_type=MESH,
        )

    def halo(x_out, y_out, x_in, y_in, phase):
        copies = []
        for d in range(4):
            src = (x_out if d < 2 else y_out).at[d % 2]
            dst = (x_in if d < 2 else y_in).at[back[d] % 2]
            copies.append((d, src, dst))

        def start():
            for d, src, dst in copies:
                sems = (halo_send.at[phase], halo_recv.at[phase])

                @pl.when(has[d])
                def _():
                    pltpu.make_async_remote_copy(
                        src_ref=src,
                        dst_ref=dst,
                        send_sem=sems[0].at[d],
                        recv_sem=sems[1].at[back[d]],
                        device_id={"col": peer[d]},
                        device_id_type=MESH,
                    ).start()

        def receive():
            for d in range(4):
                ref = (x_in if d < 2 else y_in).at[d % 2]

                @pl.when(has[d])
                def _():
                    pltpu.make_async_remote_copy(
                        src_ref=ref,
                        dst_ref=ref,
                        send_sem=halo_send.at[phase].at[d],
                        recv_sem=halo_recv.at[phase].at[d],
                        device_id={"col": peer[d]},
                        device_id_type=MESH,
                    ).wait_recv()

        def finish():
            for d, src, dst in copies:

                @pl.when(has[d])
                def _():
                    pltpu.make_async_remote_copy(
                        src_ref=src,
                        dst_ref=dst,
                        send_sem=halo_send.at[phase].at[d],
                        recv_sem=halo_recv.at[phase].at[back[d]],
                        device_id={"col": peer[d]},
                        device_id_type=MESH,
                    ).wait_send()

        return start, receive, finish

    def edges(phase):
        def copy(d):
            src = (cx_out if d < 2 else cy_out).at[phase]
            dst = (cx_in if d < 2 else cy_in).at[phase]
            slot = d // 2
            return pltpu.make_async_remote_copy(
                src_ref=src,
                dst_ref=dst,
                send_sem=edge_send.at[phase].at[slot],
                recv_sem=edge_recv.at[phase].at[slot],
                device_id={"col": peer[d]},
                device_id_type=MESH,
            )

        def start():
            for d in (1, 3):

                @pl.when(has[d])
                def _():
                    copy(d).start()

        def receive():
            for d in (0, 2):

                @pl.when(has[d])
                def _():
                    copy(d).wait_recv()

        def finish():
            for d in (1, 3):

                @pl.when(has[d])
                def _():
                    copy(d).wait_send()

        return start, receive, finish

    tall = lane_of(BLOCK)
    row = iota((probes, LANES), 0)
    wide = iota((probes, LANES), 1)

    def send_edges(ref, x_out, y_out):
        read = lambda q: ref[:, span(q)]
        x_out[0] = pack_x(read, BLOCK, 3, probes)
        x_out[1] = pack_x(read, BLOCK, 0, probes)
        y_out[0] = pack_y(read, BLOCK, TB - 1, probes)
        y_out[1] = pack_y(read, BLOCK, 0, probes)

    def spread(ref, x_in, y_in):
        for q in range(probes):
            v = ref[:, span(q)]
            parts = (
                visc * v,
                jnp.where(tall // TB == 3, unpack_x(x_in.at[0], q, 3), roll(v, -TB)),
                jnp.where(tall // TB == 0, unpack_x(x_in.at[1], q, 0), roll(v, TB)),
                jnp.where(tall % TB == TB - 1, unpack_y(y_in.at[0], q, TB - 1), roll(v, -1)),
                jnp.where(tall % TB == 0, unpack_y(y_in.at[1], q, 0), roll(v, 1)),
            )
            for i, part in enumerate(parts):
                at = slice(i * BLOCK, (i + 1) * BLOCK)
                x_h[at, span(q)], x_l[at, span(q)] = split(part)

    def apply_block(l_h, l_l):
        k = 5 * BLOCK
        return (
            dot(l_h[:, :k], x_h[...]) + dot(l_h[:, :k], x_l[...]) + dot(l_l[:, :k], x_h[...])
        )

    def column(x):
        return jnp.sum(x, axis=0, keepdims=True)

    def to_slot(which, values):
        out = jnp.zeros((probes, LANES), F32)
        for k, v in enumerate(values):
            out = jnp.where(wide == row + probes * k, jnp.sum(v, axis=1, keepdims=True), out)
        ar_ref[which, pl.ds(me, 1)] = column(out)[None]

    def from_slots(which, n):
        total = jnp.sum(ar_ref[which], axis=0)
        return [
            jnp.sum(jnp.where(wide == row + probes * k, total, 0.0), axis=1, keepdims=True)
            for k in range(n)
        ]

    reduces = [
        exchange(ar_ref.at[k], ar_ref.at[k], ar_send.at[k], ar_recv.at[k], True) for k in range(3)
    ]

    def quadratic(b_ref, first, image_ref, alpha, base_ref, phase, slot):
        for q in range(probes):
            a = alpha[q : q + 1, :]
            image_ref[:, span(q)] = -a * image_ref[:, span(q)]
            at = slice(first, first + BLOCK)
            image_ref[at, span(q)] = image_ref[at, span(q)] + b_ref[:, span(q)]
            r_h[:, span(q)], r_l[:, span(q)] = split(image_ref[:, span(q)])
        sr_ref[...] = (
            dot(s_h[:, :ROWS], r_h[...])
            + dot(s_h[:, :ROWS], r_l[...])
            + dot(s_l[:, :ROWS], r_h[...])
        )
        return edges(phase)

    def quadratic_end(image_ref, alpha, base_ref, phase, slot):
        face = lane_of(FACES)
        for q in range(probes):
            a = alpha[q : q + 1, :]
            r = image_ref[:, span(q)]
            red_ref[slot, q : q + 1, :] = column(r * r)
            t = column(visc * sr_ref[0:ROWS, span(q)] * r)
            t += column(fric16 * r[0:BLOCK] * r[0:BLOCK])
            at = ROWS
            cwr = sr_ref[at : at + FACES, span(q)]
            csr = sr_ref[at + FACES : at + 2 * FACES, span(q)]
            per = sr_ref[at + 2 * FACES : at + 3 * FACES, span(q)]
            pnr = sr_ref[at + 3 * FACES : at + 4 * FACES, span(q)]
            hx = base_ref[0:FACES, span(q)] - a * unpack_x(cx_in.at[phase], q, 3)
            hy = base_ref[FACES : 2 * FACES, span(q)] - a * unpack_y(cy_in.at[phase], q, TB - 1)
            nx = jnp.where(face // TB == 3, hx, roll(cwr, -TB))
            ny = jnp.where(face % TB == TB - 1, hy, roll(csr, -1))
            t -= 2.0 * column(per * nx + pnr * ny)
            red_ref[slot + 1, q : q + 1, :] = t

    out_receive()
    arrived = recv1[...].reshape(count * share, width)
    tile_probe = dot_exact(arrived, order, ((0,), (0,)))
    for q in range(probes):
        f_ref[:, span(q)] = -scale * tile_probe[q * BLOCK : (q + 1) * BLOCK]
    send_edges(f_ref, fx_out, fy_out)
    f_start, f_receive, f_finish = halo(fx_out, fy_out, fx_in, fy_in, 0)
    f_start()
    f_receive()
    spread(f_ref, fx_in, fy_in)
    got = apply_block(lf_h, lf_l)
    u_ref[...] = got[:ROWS]
    gf_ref[...] = got[ROWS:]
    for q in range(probes):
        u_ref[0:BLOCK, span(q)] = u_ref[0:BLOCK, span(q)] + fric16 * f_ref[:, span(q)]
        g_ref[:, span(q)] = obs16 * u_ref[TOP : TOP + BLOCK, span(q)]
    send_edges(g_ref, gx_out, gy_out)
    g_start, g_receive, g_finish = halo(gx_out, gy_out, gx_in, gy_in, 1)
    g_start()
    for q in range(probes):
        f = f_ref[:, span(q)]
        red_ref[0, q : q + 1, :] = column(f * f)
        red_ref[1, q : q + 1, :] = column(f * u_ref[0:BLOCK, span(q)])
    to_slot(0, (red_ref[0], red_ref[1]))
    reduces[0][0]()

    def compress(m, x):
        m_h, m_l = split(m)
        b_h, b_l = split(x)
        return dot(m_h, b_h) + dot(m_h, b_l) + dot(m_l, b_h)

    read_u = lambda q: u_ref[:, span(q)]
    cx_out[0] = compress(cw[:FACES, :ROWS], pack_x(read_u, ROWS, 0, probes))
    cy_out[0] = compress(cs[:FACES, :ROWS], pack_y(read_u, ROWS, 0, probes))
    u_start, u_receive, u_finish = edges(0)
    u_start()

    g_receive()
    spread(g_ref, gx_in, gy_in)
    got = apply_block(lg_h, lg_l)
    w_ref[...] = got[:ROWS]
    gg_ref[...] = got[ROWS : ROWS + 2 * FACES]
    sr_ref[0 : 2 * FACES, :] = got[ROWS + 2 * FACES :]
    cx_out[1] = pack_x(lambda q: sr_ref[0:FACES, span(q)], FACES, 0, probes)
    cy_out[1] = pack_y(lambda q: sr_ref[FACES : 2 * FACES, span(q)], FACES, 0, probes)
    w_start, w_receive, w_finish = edges(1)
    w_start()
    for q in range(probes):
        g = g_ref[:, span(q)]
        red_ref[0, q : q + 1, :] = column(g * g)
        red_ref[1, q : q + 1, :] = column(g * w_ref[TOP : TOP + BLOCK, span(q)])
    to_slot(1, (red_ref[0], red_ref[1]))
    reduces[1][0]()

    reduces[0][1]()
    rr0, dad0 = from_slots(0, 2)
    alpha0 = rr0 / dad0
    quadratic(f_ref, 0, u_ref, alpha0, gf_ref, 0, 0)
    u_receive()
    quadratic_end(u_ref, alpha0, gf_ref, 0, 0)

    reduces[1][1]()
    qq0, ded0 = from_slots(1, 2)
    gamma0 = qq0 / ded0
    quadratic(g_ref, TOP, w_ref, gamma0, gg_ref, 1, 2)
    w_receive()
    quadratic_end(w_ref, gamma0, gg_ref, 1, 2)
    to_slot(2, tuple(red_ref[k] for k in range(4)))
    reduces[2][0]()
    reduces[2][1]()
    rr1, rar, qq1, qaq = from_slots(2, 4)
    beta = rr1 / rr0
    alpha1 = rr1 / (rar - beta * beta * dad0)
    delta = qq1 / qq0
    gamma1 = qq1 / (qaq - delta * delta * ded0)
    factor = alpha0 * alpha1
    on_b = factor * (gamma0 + gamma1 * delta)
    on_r = factor * gamma1

    for q in range(probes):
        act_ref[q * BLOCK : (q + 1) * BLOCK, :] = (
            scale * on_r[q : q + 1, :] * w_ref[0:BLOCK, span(q)]
        )
    placed = dot_exact(order, act_ref[...], ((1,), (1,)))
    send2[...] = placed.reshape(count, share, width)
    recv2[pl.ds(me, 1)] = send2[pl.ds(me, 1)]
    home_start, home_receive, home_finish = exchange(
        send2, recv2, a2a_send.at[1], a2a_recv.at[1], False
    )
    home_start()
    for q in range(probes):
        w_ref[:, span(q)] = on_r[q : q + 1, :] * w_ref[:, span(q)]
        at = slice(TOP, TOP + BLOCK)
        w_ref[at, span(q)] = w_ref[at, span(q)] + on_b[q : q + 1, :] * g_ref[:, span(q)]
        adj_ref[:, q, :] = w_ref[0:DOF, span(q)]
    out_finish()
    f_finish()
    g_finish()
    u_finish()
    w_finish()
    for k in range(3):
        reduces[k][2]()
    home_receive()
    hess = recv2[...].reshape(count * share, width).T
    for q in range(probes):
        hess_ref[:, q, :] = hess[q * BLOCK : q * BLOCK + BASAL]
    home_finish()


def local(
    base_velocity,
    viscosity,
    friction,
    obs_weight,
    stiffness,
    face_coupling,
    face_rows,
    tile_source,
    probes,
):
    count = lax.axis_size("col")
    tiles = viscosity.shape[0]
    depth, number = probes.shape[0], probes.shape[1]
    share = tiles // count
    full = number * tiles
    width = number * BLOCK
    quarter = number // 4 * LANES
    vm = pltpu.VMEM
    dma = pltpu.SemaphoreType.DMA
    scratch = [
        vm((LANES, LANES), F32),
        vm((8, LANES), jnp.int32),
        vm((BLOCK, LANES), F32),
        vm((BLOCK, LANES), F32),
        vm((BLOCK, LANES), F32),
        vm((ROWS + 2 * FACES, LANES), BF16),
        vm((ROWS + 2 * FACES, LANES), BF16),
        vm((ROWS + 4 * FACES, LANES), BF16),
        vm((ROWS + 4 * FACES, LANES), BF16),
        vm((ROWS + 4 * FACES, LANES), BF16),
        vm((ROWS + 4 * FACES, LANES), BF16),
        vm((BLOCK, full), F32),
        vm((BLOCK, full), F32),
        vm((ROWS, full), F32),
        vm((ROWS, full), F32),
        vm((2 * FACES, full), F32),
        vm((2 * FACES, full), F32),
        vm((5 * BLOCK, full), BF16),
        vm((5 * BLOCK, full), BF16),
        vm((ROWS, full), BF16),
        vm((ROWS, full), BF16),
        vm((ROWS + 4 * FACES, full), F32),
        vm((width, LANES), F32),
        vm((4, number, LANES), F32),
        vm((count, share, width), F32),
        vm((count, share, width), F32),
        vm((count, share, width), F32),
        vm((count, share, width), F32),
        vm((3, count, 1, LANES), F32),
        vm((2, BLOCK, quarter), F32),
        vm((2, BLOCK, LANES), F32),
        vm((2, BLOCK, quarter), F32),
        vm((2, BLOCK, LANES), F32),
        vm((2, BLOCK, quarter), F32),
        vm((2, BLOCK, LANES), F32),
        vm((2, BLOCK, quarter), F32),
        vm((2, BLOCK, LANES), F32),
        vm((2, FACES, quarter), F32),
        vm((2, FACES, LANES), F32),
        vm((2, FACES, quarter), F32),
        vm((2, FACES, LANES), F32),
        dma((2, count)),
        dma((2, count)),
        dma((3, count)),
        dma((3, count)),
        dma((2, 4)),
        dma((2, 4)),
        dma((2, 2)),
        dma((2, 2)),
    ]
    return pl.pallas_call(
        functools.partial(kernel, count, number),
        out_shape=(
            jax.ShapeDtypeStruct((depth, number, tiles), F32),
            jax.ShapeDtypeStruct((DOF, number, tiles), F32),
        ),
        in_specs=[pl.BlockSpec(memory_space=pltpu.VMEM)] * 9,
        out_specs=(pl.BlockSpec(memory_space=pltpu.VMEM),) * 2,
        scratch_shapes=scratch,
        compiler_params=pltpu.CompilerParams(
            collective_id=0, has_side_effects=True, vmem_limit_bytes=48 * 1024 * 1024
        ),
    )(
        base_velocity,
        viscosity[None, :],
        friction,
        obs_weight,
        stiffness,
        face_coupling,
        face_rows,
        tile_source,
        probes,
    )


def solution(mesh):
    placed = (
        P(None, ("grp", "col")),
        P(("grp", "col")),
        P(None, ("grp", "col")),
        P(None, ("grp", "col")),
        P(),
        P(),
        P(),
        P("col", None),
        P(None, None, ("grp", "col")),
    )
    return jax.shard_map(
        local,
        mesh=mesh,
        in_specs=placed,
        out_specs=(P(None, None, ("grp", "col")), P(None, None, ("grp", "col"))),
        check_vma=False,
    )
```

time: 566 us -> 46 us (0.08); the launches traced: 557 us -> 45.5 us
  blocking collectives: 186 us -> 0 us
  local copies, waits for them, and re-layouts: 191 us -> 7.38 us
  other arithmetic: 95.6 us -> 0 us
  starting transfers between devices: 48.6 us -> 0 us
  Pallas kernels: 0 us -> 37.5 us
  matrix products: 25.3 us -> 0 us
  waiting for transfers between devices: 8.03 us -> 0 us
    psum x6 -> x0, blocking collectives: 186 us -> none  [the longest x4 123 us: square_total(): return lax.psum(local_sum(resid, resid), 'col')[None, :, None]]
    scatter-add x16 -> x0, other arithmetic: 60.8 us -> none  [the longest x4 15.9 us: couple_local(): total = total.at[east].add(-to_east)]
    gather x50 -> x0, local copies, waits for them, and re-layouts: 40.8 us -> none  [the longest x4 6.71 us: couple_local(): north_vals = jnp.take(grid, north, axis=0)]
    ppermute x16 -> x0, starting transfers between devices: 37.7 us -> none  [from_behind(): return lax.ppermute(value, axis, pairs)]
    pallas_call x0 -> x1, Pallas kernels: none -> 37.5 us  [local(): pl.pallas_call(functools.partial(kernel, count, number), out_shape=(jax.S...]
    neg x18 -> x0, local copies, waits for them, and re-layouts: 33 us -> none  [the longest x4 10.5 us: couple_local(): total = total.at[south].add(-to_south)]
    unnamed x156 -> x20, local copies, waits for them, and re-layouts: 39.7 us -> 7.38 us
    dot_general x20 -> x0, matrix products: 25.3 us -> none  [the longest x4 6.95 us: couple_local(): jnp.einsum('gf,gqab->fqab', face_coupling, north_prev, precision=lax.Prec...]
  transfers between devices with their start and end apart: 18 -> 0, of which waited for: 2 -> 0; matrix products, arithmetic and copies ran while one was open for 21% -> 0% of each run, Pallas kernels for 0% -> 0%
where the time goes in v1:
time: 46 us; the launch traced here: 45.5 us
  Pallas kernels  37.5 us (82%)
  local copies, waits for them, and re-layouts  7.38 us (16%)
  between operations  0.67 us (1%)
    pallas_call x1, Pallas kernels, local(): pl.pallas_call(functools.partial(kernel, count, number), out_shape=(jax.S...  37.5 us
    unnamed x20, local copies, waits for them, and re-layouts  7.38 us

profile of v1, /device:TPU:0, one launch (start us, length us, event | category | flops | bytes accessed | tf_op | source)
XLA Modules:
  0.0 45.5 jit_solution(8182458480866913057)
XLA Ops:
  0.6 0.0 copy-start.8
  0.6 0.0 copy-start.7
  0.7 0.6 %copy-done.8 = s32[1,128]{1,0:T(1,128)S(1)} copy-done((s32[1,128]{1,0:T(1,128)S(1)}, s32[1,128]{1,0:T(1,128)}, u32[]{:S(2)}) %copy-start.8) | copy-done | bytes 536
  1.3 0.0 copy-done.7
  1.3 0.0 copy-start
  1.3 0.9 %copy-done = f32[9,16,128]{2,1,0:T(8,128)S(1)} copy-done((f32[9,16,128]{2,1,0:T(8,128)S(1)}, f32[9,16,128]{2,1,0:T(8,128)}, u32[]{:S(2)}) %copy-start) | copy-done | bytes 73752
  2.2 0.0 copy-start.1
  2.2 0.8 %copy-done.1 = f32[81,128]{1,0:T(8,128)S(1)} copy-done((f32[81,128]{1,0:T(8,128)S(1)}, f32[81,128]{1,0:T(8,128)}, u32[]{:S(2)}) %copy-start.1) | copy-done | bytes 41496
  3.0 0.0 copy-start.2
  3.0 0.8 %copy-done.2 = f32[81,81]{1,0:T(8,128)S(1)} copy-done((f32[81,81]{1,0:T(8,128)S(1)}, f32[81,81]{1,0:T(8,128)}, u32[]{:S(2)}) %copy-start.2) | copy-done | bytes 26268
  3.8 0.0 copy-start.3
  3.8 0.7 %copy-done.3 = f32[27,27]{1,0:T(8,128)S(1)} copy-done((f32[27,27]{1,0:T(8,128)S(1)}, f32[27,27]{1,0:T(8,128)}, u32[]{:S(2)}) %copy-start.3) | copy-done | bytes 2940
  4.5 0.0 copy-start.4
  4.5 0.7 %copy-done.4 = f32[9,128]{1,0:T(8,128)S(1)} copy-done((f32[9,128]{1,0:T(8,128)S(1)}, f32[9,128]{1,0:T(8,128)}, u32[]{:S(2)}) %copy-start.4) | copy-done | bytes 4632
  5.2 0.0 copy-start.5
  5.2 0.7 %copy-done.5 = f32[9,128]{1,0:T(8,128)S(1)} copy-done((f32[9,128]{1,0:T(8,128)S(1)}, f32[9,128]{1,0:T(8,128)}, u32[]{:S(2)}) %copy-start.5) | copy-done | bytes 4632
  5.9 0.0 copy-start.6
  5.9 0.7 %copy-done.6 = s32[4,27]{1,0:T(4,128)S(1)} copy-done((s32[4,27]{1,0:T(4,128)S(1)}, s32[4,27]{1,0:T(4,128)}, u32[]{:S(2)}) %copy-start.6) | copy-done | bytes 456
  6.6 37.5 %shard_map.104 = (f32[9,16,128]{2,1,0:T(8,128)S(1)}, f32[81,16,128]{2,1,0:T(8,128)S(1)}) custom-call(f32[81,128]{1,0:T(8,128)S(1)} %copy-done.1, f32[1,128]{1,0:T(1,128)S(1)} %bitcast.1, f32[9,128]{1,0:T(8,128)S(1)} %copy-done.4, f32[9,128]{1,0:T(8,128)S(1)} %copy-done.5, f32[81,81]{1,0:T(8,128)S(1)} %copy-done.2, f32[27,27]{1,0:T(8,128)S(1)} %copy-done.3, ...), custom_call_target="tpu_custom_call" | custom-call | tf_op jit(solution)/shard_map/pallas_call | solution.py:658
  44.1 0.6 %copy.13 = f32[9,16,128]{2,1,0:T(8,128)} copy(f32[9,16,128]{2,1,0:T(8,128)S(1)} %get-tuple-element.4) | data formatting | bytes 147456
  44.7 0.8 %copy.14 = f32[81,16,128]{2,1,0:T(8,128)} copy(f32[81,16,128]{2,1,0:T(8,128)S(1)} %get-tuple-element.5) | data formatting | bytes 1327104
Async XLA Ops:
  0.6 0.7 %copy-start.8 = (s32[1,128]{1,0:T(1,128)S(1)}, s32[1,128]{1,0:T(1,128)}, u32[]{:S(2)}) copy-start(s32[1,128]{1,0:T(1,128)} %source_ref.1) | copy-start | bytes 1540
  0.6 0.7 %copy-start.7 = (f32[128]{0:T(128)S(1)}, f32[128]{0:T(128)}, u32[]{:S(2)}) copy-start(f32[128]{0:T(128)} %param.10) | copy-start | bytes 1540
  1.3 0.9 %copy-start = (f32[9,16,128]{2,1,0:T(8,128)S(1)}, f32[9,16,128]{2,1,0:T(8,128)}, u32[]{:S(2)}) copy-start(f32[9,16,128]{2,1,0:T(8,128)} %probes_ref.1) | copy-start | bytes 221188
  2.2 0.8 %copy-start.1 = (f32[81,128]{1,0:T(8,128)S(1)}, f32[81,128]{1,0:T(8,128)}, u32[]{:S(2)}) copy-start(f32[81,128]{1,0:T(8,128)} %vel_ref.1) | copy-start | bytes 124420
  3.0 0.8 %copy-start.2 = (f32[81,81]{1,0:T(8,128)S(1)}, f32[81,81]{1,0:T(8,128)}, u32[]{:S(2)}) copy-start(f32[81,81]{1,0:T(8,128)} %stiff_ref.1) | copy-start | bytes 78736
  3.8 0.7 %copy-start.3 = (f32[27,27]{1,0:T(8,128)S(1)}, f32[27,27]{1,0:T(8,128)}, u32[]{:S(2)}) copy-start(f32[27,27]{1,0:T(8,128)} %coup_ref.1) | copy-start | bytes 8752
  4.5 0.7 %copy-start.4 = (f32[9,128]{1,0:T(8,128)S(1)}, f32[9,128]{1,0:T(8,128)}, u32[]{:S(2)}) copy-start(f32[9,128]{1,0:T(8,128)} %fric_ref.1) | copy-start | bytes 13828
  5.2 0.7 %copy-start.5 = (f32[9,128]{1,0:T(8,128)S(1)}, f32[9,128]{1,0:T(8,128)}, u32[]{:S(2)}) copy-start(f32[9,128]{1,0:T(8,128)} %obs_ref.1) | copy-start | bytes 13828
  5.9 0.7 %copy-start.6 = (s32[4,27]{1,0:T(4,128)S(1)}, s32[4,27]{1,0:T(4,128)}, u32[]{:S(2)}) copy-start(s32[4,27]{1,0:T(4,128)} %faces_ref.1) | copy-start | bytes 1300

commit v2 on v1

--- a/solution.py
+++ b/solution.py
@@ -82,6 +82,17 @@
 def kernel(
     count,
     probes,
+    vel_hbm,
+    visc_hbm,
+    fric_hbm,
+    obs_hbm,
+    stiff_hbm,
+    coup_hbm,
+    faces_hbm,
+    source_hbm,
+    probes_hbm,
+    hess_ref,
+    adj_ref,
     vel_ref,
     visc_ref,
     fric_ref,
@@ -91,8 +102,7 @@
     faces_ref,
     source_ref,
     probes_ref,
-    hess_ref,
-    adj_ref,
+    load_sem,
     pad_ref,
     fpad_ref,
     scale_ref,
@@ -155,17 +165,46 @@
 
     barrier = pltpu.get_barrier_semaphore()
 
-    def greet(o, carry):
-        pl.semaphore_signal(
-            barrier, inc=1, device_id={"col": lax.rem(me + o, count)}, device_id_type=MESH
+    def others(act):
+        def one(o):
+            other = me + o
+            act(jnp.where(other < count, other, other - count))
+
+        if count <= 16:
+            for o in range(1, count):
+                one(o)
+        else:
+
+            def body(o, carry):
+                one(o)
+                return carry
+
+            lax.fori_loop(1, count, body, 0)
+
+    pairs = (
+        (probes_hbm, probes_ref),
+        (stiff_hbm, stiff_ref),
+        (coup_hbm, coup_ref),
+        (faces_hbm, faces_ref),
+        (vel_hbm.at[0:BLOCK], vel_ref),
+        (fric_hbm, fric_ref),
+        (obs_hbm, obs_ref),
+        (source_hbm, source_ref),
+        (visc_hbm, visc_ref),
+    )
+    loads = [pltpu.make_async_copy(a, b, load_sem.at[k]) for k, (a, b) in enumerate(pairs)]
+    for load in loads:
+        load.start()
+    others(
+        lambda other: pl.semaphore_signal(
+            barrier, inc=1, device_id={"col": other}, device_id_type=MESH
         )
-        return carry
-
-    lax.fori_loop(1, count, greet, 0)
+    )
 
     for buf in (fx_in, fy_in, gx_in, gy_in, cx_in, cy_in):
         buf[...] = jnp.zeros_like(buf)
     rows = []
+    loads[0].wait()
     pad_ref[...] = jnp.zeros_like(pad_ref)
     for q in range(probes):
         pad_ref[0:BASAL, :] = probes_ref[:, q, :]
@@ -179,44 +218,34 @@
     pl.semaphore_wait(barrier, count - 1)
 
     def exchange(src, dst, send_sem, recv_sem, own):
-        def one(o):
-            other = lax.rem(me + o, count)
-            return pltpu.make_async_remote_copy(
-                src_ref=src.at[me if own else other],
-                dst_ref=dst.at[me],
-                send_sem=send_sem.at[other],
-                recv_sem=recv_sem.at[me],
-                device_id={"col": other},
-                device_id_type=MESH,
+        def start():
+            others(
+                lambda other: pltpu.make_async_remote_copy(
+                    src_ref=src.at[me if own else other],
+                    dst_ref=dst.at[me],
+                    send_sem=send_sem,
+                    recv_sem=recv_sem,
+                    device_id={"col": other},
+                    device_id_type=MESH,
+                ).start()
             )
 
-        def arrival(o):
-            other = lax.rem(me + o, count)
-            return pltpu.make_async_remote_copy(
-                src_ref=src.at[me if own else other],
-                dst_ref=dst.at[other],
-                send_sem=send_sem.at[other],
-                recv_sem=recv_sem.at[other],
-                device_id={"col": other},
-                device_id_type=MESH,
-            )
-
-        def loop(act):
-            def body(o, carry):
-                act(o)
-                return carry
-
-            lax.fori_loop(1, count, body, 0)
-
-        start = lambda: loop(lambda o: one(o).start())
-        receive = lambda: loop(lambda o: arrival(o).wait_recv())
-        finish = lambda: loop(lambda o: one(o).wait_send())
+        rest = pl.ds(0, count - 1)
+
+        def receive():
+            pltpu.make_async_copy(dst.at[rest], dst.at[rest], recv_sem).wait()
+
+        def finish():
+            pltpu.make_async_copy(src.at[rest], src.at[rest], send_sem).wait()
+
         return start, receive, finish
 
     out_start, out_receive, out_finish = exchange(
         send1, recv1, a2a_send.at[0], a2a_recv.at[0], False
     )
     out_start()
+    for load in loads[1:]:
+        load.wait()
 
     def padded(ref, height, width_):
         pad_ref[...] = jnp.zeros_like(pad_ref)
@@ -528,6 +557,15 @@
         red_ref[1, q : q + 1, :] = column(g * w_ref[TOP : TOP + BLOCK, span(q)])
     to_slot(1, (red_ref[0], red_ref[1]))
     reduces[1][0]()
+    for q in range(probes):
+        act_ref[q * BLOCK : (q + 1) * BLOCK, :] = scale * w_ref[0:BLOCK, span(q)]
+    placed = dot_exact(order, act_ref[...], ((1,), (1,)))
+    send2[...] = placed.reshape(count, share, width)
+    recv2[pl.ds(me, 1)] = send2[pl.ds(me, 1)]
+    home_start, home_receive, home_finish = exchange(
+        send2, recv2, a2a_send.at[1], a2a_recv.at[1], False
+    )
+    home_start()
 
     reduces[0][1]()
     rr0, dad0 = from_slots(0, 2)
@@ -553,18 +591,8 @@
     factor = alpha0 * alpha1
     on_b = factor * (gamma0 + gamma1 * delta)
     on_r = factor * gamma1
-
-    for q in range(probes):
-        act_ref[q * BLOCK : (q + 1) * BLOCK, :] = (
-            scale * on_r[q : q + 1, :] * w_ref[0:BLOCK, span(q)]
-        )
-    placed = dot_exact(order, act_ref[...], ((1,), (1,)))
-    send2[...] = placed.reshape(count, share, width)
-    recv2[pl.ds(me, 1)] = send2[pl.ds(me, 1)]
-    home_start, home_receive, home_finish = exchange(
-        send2, recv2, a2a_send.at[1], a2a_recv.at[1], False
-    )
-    home_start()
+    on_w = -on_r * gamma0
+
     for q in range(probes):
         w_ref[:, span(q)] = on_r[q : q + 1, :] * w_ref[:, span(q)]
         at = slice(TOP, TOP + BLOCK)
@@ -580,7 +608,7 @@
     home_receive()
     hess = recv2[...].reshape(count * share, width).T
     for q in range(probes):
-        hess_ref[:, q, :] = hess[q * BLOCK : q * BLOCK + BASAL]
+        hess_ref[:, q, :] = on_w[q : q + 1, :] * hess[q * BLOCK : q * BLOCK + BASAL]
     home_finish()
 
 
@@ -605,6 +633,16 @@
     vm = pltpu.VMEM
     dma = pltpu.SemaphoreType.DMA
     scratch = [
+        vm((BLOCK, tiles), F32),
+        vm((1, tiles), F32),
+        vm(friction.shape, F32),
+        vm(obs_weight.shape, F32),
+        vm(stiffness.shape, F32),
+        vm(face_coupling.shape, F32),
+        vm(face_rows.shape, jnp.int32),
+        vm(tile_source.shape, jnp.int32),
+        vm(probes.shape, F32),
+        dma((9,)),
         vm((LANES, LANES), F32),
         vm((8, LANES), jnp.int32),
         vm((BLOCK, LANES), F32),
@@ -646,10 +684,10 @@
         vm((2, FACES, LANES), F32),
         vm((2, FACES, quarter), F32),
         vm((2, FACES, LANES), F32),
-        dma((2, count)),
-        dma((2, count)),
-        dma((3, count)),
-        dma((3, count)),
+        dma((2,)),
+        dma((2,)),
+        dma((3,)),
+        dma((3,)),
         dma((2, 4)),
         dma((2, 4)),
         dma((2, 2)),
@@ -661,7 +699,7 @@
             jax.ShapeDtypeStruct((depth, number, tiles), F32),
             jax.ShapeDtypeStruct((DOF, number, tiles), F32),
         ),
-        in_specs=[pl.BlockSpec(memory_space=pltpu.VMEM)] * 9,
+        in_specs=[pl.BlockSpec(memory_space=pltpu.HBM)] * 9,
         out_specs=(pl.BlockSpec(memory_space=pltpu.VMEM),) * 2,
         scratch_shapes=scratch,
         compiler_params=pltpu.CompilerParams(

time: 46 us -> 39.3 us (0.85)
  Pallas kernels: 37.5 us -> 30.8 us
    pallas_call x1, Pallas kernels: 37.5 us -> 30.8 us  [local(): pl.pallas_call(functools.partial(kernel, count, number), out_shape=(jax.S...]
where the time goes in v2:
time: 39.3 us; the launch traced here: 38.9 us
  Pallas kernels  30.8 us (78%)
  local copies, waits for them, and re-layouts  7.38 us (19%)
  between operations  0.67 us (2%)
    pallas_call x1, Pallas kernels, local(): pl.pallas_call(functools.partial(kernel, count, number), out_shape=(jax.S...  30.8 us
    unnamed x20, local copies, waits for them, and re-layouts  7.38 us

profile of v2, /device:TPU:0, one launch (start us, length us, event | category | flops | bytes accessed | tf_op | source)
XLA Modules:
  0.0 38.9 jit_solution(8267916355164317533)
XLA Ops:
  0.6 0.0 copy-start.8
  0.6 0.0 copy-start.7
  0.7 0.6 %copy-done.8 = s32[1,128]{1,0:T(1,128)S(1)} copy-done((s32[1,128]{1,0:T(1,128)S(1)}, s32[1,128]{1,0:T(1,128)}, u32[]{:S(2)}) %copy-start.8) | copy-done | bytes 536
  1.3 0.0 copy-done.7
  1.3 0.0 copy-start
  1.3 0.9 %copy-done = f32[9,16,128]{2,1,0:T(8,128)S(1)} copy-done((f32[9,16,128]{2,1,0:T(8,128)S(1)}, f32[9,16,128]{2,1,0:T(8,128)}, u32[]{:S(2)}) %copy-start) | copy-done | bytes 73752
  2.2 0.0 copy-start.1
  2.2 0.8 %copy-done.1 = f32[81,128]{1,0:T(8,128)S(1)} copy-done((f32[81,128]{1,0:T(8,128)S(1)}, f32[81,128]{1,0:T(8,128)}, u32[]{:S(2)}) %copy-start.1) | copy-done | bytes 41496
  3.0 0.0 copy-start.2
  3.0 0.8 %copy-done.2 = f32[81,81]{1,0:T(8,128)S(1)} copy-done((f32[81,81]{1,0:T(8,128)S(1)}, f32[81,81]{1,0:T(8,128)}, u32[]{:S(2)}) %copy-start.2) | copy-done | bytes 26268
  3.8 0.0 copy-start.3
  3.8 0.7 %copy-done.3 = f32[27,27]{1,0:T(8,128)S(1)} copy-done((f32[27,27]{1,0:T(8,128)S(1)}, f32[27,27]{1,0:T(8,128)}, u32[]{:S(2)}) %copy-start.3) | copy-done | bytes 2940
  4.5 0.0 copy-start.4
  4.5 0.7 %copy-done.4 = f32[9,128]{1,0:T(8,128)S(1)} copy-done((f32[9,128]{1,0:T(8,128)S(1)}, f32[9,128]{1,0:T(8,128)}, u32[]{:S(2)}) %copy-start.4) | copy-done | bytes 4632
  5.2 0.0 copy-start.5
  5.2 0.7 %copy-done.5 = f32[9,128]{1,0:T(8,128)S(1)} copy-done((f32[9,128]{1,0:T(8,128)S(1)}, f32[9,128]{1,0:T(8,128)}, u32[]{:S(2)}) %copy-start.5) | copy-done | bytes 4632
  5.9 0.0 copy-start.6
  5.9 0.7 %copy-done.6 = s32[4,27]{1,0:T(4,128)S(1)} copy-done((s32[4,27]{1,0:T(4,128)S(1)}, s32[4,27]{1,0:T(4,128)}, u32[]{:S(2)}) %copy-start.6) | copy-done | bytes 456
  6.6 30.8 %shard_map.104 = (f32[9,16,128]{2,1,0:T(8,128)S(1)}, f32[81,16,128]{2,1,0:T(8,128)S(1)}) custom-call(f32[81,128]{1,0:T(8,128)S(1)} %copy-done.1, f32[1,128]{1,0:T(1,128)S(1)} %bitcast.1, f32[9,128]{1,0:T(8,128)S(1)} %copy-done.4, f32[9,128]{1,0:T(8,128)S(1)} %copy-done.5, f32[81,81]{1,0:T(8,128)S(1)} %copy-done.2, f32[27,27]{1,0:T(8,128)S(1)} %copy-done.3, ...), custom_call_target="tpu_custom_call" | custom-call | tf_op jit(solution)/shard_map/pallas_call | solution.py:696
  37.4 0.6 %copy.13 = f32[9,16,128]{2,1,0:T(8,128)} copy(f32[9,16,128]{2,1,0:T(8,128)S(1)} %get-tuple-element.4) | data formatting | bytes 147456
  38.1 0.8 %copy.14 = f32[81,16,128]{2,1,0:T(8,128)} copy(f32[81,16,128]{2,1,0:T(8,128)S(1)} %get-tuple-element.5) | data formatting | bytes 1327104
Async XLA Ops:
  0.6 0.7 %copy-start.8 = (s32[1,128]{1,0:T(1,128)S(1)}, s32[1,128]{1,0:T(1,128)}, u32[]{:S(2)}) copy-start(s32[1,128]{1,0:T(1,128)} %source_hbm.1) | copy-start | bytes 1540
  0.6 0.7 %copy-start.7 = (f32[128]{0:T(128)S(1)}, f32[128]{0:T(128)}, u32[]{:S(2)}) copy-start(f32[128]{0:T(128)} %param.10) | copy-start | bytes 1540
  1.3 0.9 %copy-start = (f32[9,16,128]{2,1,0:T(8,128)S(1)}, f32[9,16,128]{2,1,0:T(8,128)}, u32[]{:S(2)}) copy-start(f32[9,16,128]{2,1,0:T(8,128)} %probes_hbm.1) | copy-start | bytes 221188
  2.2 0.8 %copy-start.1 = (f32[81,128]{1,0:T(8,128)S(1)}, f32[81,128]{1,0:T(8,128)}, u32[]{:S(2)}) copy-start(f32[81,128]{1,0:T(8,128)} %vel_hbm.1) | copy-start | bytes 124420
  3.0 0.8 %copy-start.2 = (f32[81,81]{1,0:T(8,128)S(1)}, f32[81,81]{1,0:T(8,128)}, u32[]{:S(2)}) copy-start(f32[81,81]{1,0:T(8,128)} %stiff_hbm.1) | copy-start | bytes 78736
  3.8 0.7 %copy-start.3 = (f32[27,27]{1,0:T(8,128)S(1)}, f32[27,27]{1,0:T(8,128)}, u32[]{:S(2)}) copy-start(f32[27,27]{1,0:T(8,128)} %coup_hbm.1) | copy-start | bytes 8752
  4.5 0.7 %copy-start.4 = (f32[9,128]{1,0:T(8,128)S(1)}, f32[9,128]{1,0:T(8,128)}, u32[]{:S(2)}) copy-start(f32[9,128]{1,0:T(8,128)} %fric_hbm.1) | copy-start | bytes 13828
  5.2 0.7 %copy-start.5 = (f32[9,128]{1,0:T(8,128)S(1)}, f32[9,128]{1,0:T(8,128)}, u32[]{:S(2)}) copy-start(f32[9,128]{1,0:T(8,128)} %obs_hbm.1) | copy-start | bytes 13828
  5.9 0.7 %copy-start.6 = (s32[4,27]{1,0:T(4,128)S(1)}, s32[4,27]{1,0:T(4,128)}, u32[]{:S(2)}) copy-start(s32[4,27]{1,0:T(4,128)} %faces_hbm.1) | copy-start | bytes 1300

commit v3 on v2

--- a/solution.py
+++ b/solution.py
@@ -557,6 +557,13 @@
         red_ref[1, q : q + 1, :] = column(g * w_ref[TOP : TOP + BLOCK, span(q)])
     to_slot(1, (red_ref[0], red_ref[1]))
     reduces[1][0]()
+    reduces[0][1]()
+    rr0, dad0 = from_slots(0, 2)
+    alpha0 = rr0 / dad0
+    quadratic(f_ref, 0, u_ref, alpha0, gf_ref, 0, 0)
+    u_receive()
+    quadratic_end(u_ref, alpha0, gf_ref, 0, 0)
+
     for q in range(probes):
         act_ref[q * BLOCK : (q + 1) * BLOCK, :] = scale * w_ref[0:BLOCK, span(q)]
     placed = dot_exact(order, act_ref[...], ((1,), (1,)))
@@ -566,13 +573,6 @@
         send2, recv2, a2a_send.at[1], a2a_recv.at[1], False
     )
     home_start()
-
-    reduces[0][1]()
-    rr0, dad0 = from_slots(0, 2)
-    alpha0 = rr0 / dad0
-    quadratic(f_ref, 0, u_ref, alpha0, gf_ref, 0, 0)
-    u_receive()
-    quadratic_end(u_ref, alpha0, gf_ref, 0, 0)
 
     reduces[1][1]()
     qq0, ded0 = from_slots(1, 2)
@@ -693,6 +693,17 @@
         dma((2, 2)),
         dma((2, 2)),
     ]
+    operands = (
+        base_velocity,
+        viscosity[None, :],
+        friction,
+        obs_weight,
+        stiffness,
+        face_coupling,
+        face_rows,
+        tile_source,
+        probes,
+    )
     return pl.pallas_call(
         functools.partial(kernel, count, number),
         out_shape=(
@@ -705,17 +716,7 @@
         compiler_params=pltpu.CompilerParams(
             collective_id=0, has_side_effects=True, vmem_limit_bytes=48 * 1024 * 1024
         ),
-    )(
-        base_velocity,
-        viscosity[None, :],
-        friction,
-        obs_weight,
-        stiffness,
-        face_coupling,
-        face_rows,
-        tile_source,
-        probes,
-    )
+    )(*(pltpu.with_memory_space_constraint(x, pltpu.HBM) for x in operands))
 
 
 def solution(mesh):

time: 39.3 us -> 32.7 us (0.83)
  local copies, waits for them, and re-layouts: 7.38 us -> 1.47 us
    unnamed x20 -> x2, local copies, waits for them, and re-layouts: 7.38 us -> 1.47 us
where the time goes in v3:
time: 32.7 us; the launch traced here: 32.6 us
  Pallas kernels  30.5 us (93%)
  local copies, waits for them, and re-layouts  1.47 us (4%)
  between operations  0.64 us (2%)
    pallas_call x1, Pallas kernels, local(): pl.pallas_call(functools.partial(kernel, count, number), out_shape=(jax.S...  30.5 us
    unnamed x2, local copies, waits for them, and re-layouts  1.47 us

profile of v3, /device:TPU:0, one launch (start us, length us, event | category | flops | bytes accessed | tf_op | source)
XLA Modules:
  0.0 32.6 jit_solution(4715295016981907934)
XLA Ops:
  0.6 30.5 %shard_map.104 = (f32[9,16,128]{2,1,0:T(8,128)S(1)}, f32[81,16,128]{2,1,0:T(8,128)S(1)}) custom-call(f32[81,128]{1,0:T(8,128)} %vel_hbm.1, f32[1,128]{1,0:T(1,128)} %bitcast.1, f32[9,128]{1,0:T(8,128)} %fric_hbm.1, f32[9,128]{1,0:T(8,128)} %obs_hbm.1, f32[81,81]{1,0:T(8,128)} %stiff_hbm.1, f32[27,27]{1,0:T(8,128)} %coup_hbm.1, s32[4,27]{1,0:T(4,128)} %faces_hbm.1, ...), custom_call_target="tpu_custom_call" | custom-call | tf_op jit(solution)/shard_map/pallas_call | solution.py:707
  31.1 0.6 %copy.13 = f32[9,16,128]{2,1,0:T(8,128)} copy(f32[9,16,128]{2,1,0:T(8,128)S(1)} %get-tuple-element.4) | data formatting | bytes 147456
  31.7 0.8 %copy.14 = f32[81,16,128]{2,1,0:T(8,128)} copy(f32[81,16,128]{2,1,0:T(8,128)S(1)} %get-tuple-element.5) | data formatting | bytes 1327104

commit v4 on v3

--- a/solution.py
+++ b/solution.py
@@ -13,6 +13,8 @@
 LANES = 128
 TOP = 72
 ROWS = 96
+HEAD = 80
+DEPTH = 256
 BLOCK = 16
 FACES = 32
 F32 = jnp.float32
@@ -29,6 +31,19 @@
 def split(x):
     high = x.astype(BF16)
     return high, (x - high.astype(F32)).astype(BF16)
+
+
+def stacked(m):
+    high = m.astype(BF16).astype(F32)
+    low = m - high
+    lane = lane_of(m.shape[0])
+    left = jnp.where(lane < HEAD, high, roll(high, HEAD))
+    right = jnp.where(lane < 32, roll(high, HEAD), roll(low, 32))
+    right = jnp.where(lane == 112, roll(high, 32), right)
+    right = jnp.where(lane == 113, roll(high, 33), right)
+    right = jnp.where(lane == 114, roll(low, 34), right)
+    right = jnp.where(lane > 114, 0.0, right)
+    return jnp.concatenate([left, right], axis=1).astype(BF16)
 
 
 def dot(a, b):
@@ -108,22 +123,18 @@
     scale_ref,
     fric16_ref,
     obs16_ref,
-    lf_h,
-    lf_l,
-    lg_h,
-    lg_l,
-    s_h,
-    s_l,
+    lf_ref,
+    lg_ref,
+    s_ref,
+    adjg_ref,
     f_ref,
     g_ref,
     u_ref,
     w_ref,
     gf_ref,
     gg_ref,
-    x_h,
-    x_l,
-    r_h,
-    r_l,
+    x_ref,
+    r_ref,
     sr_ref,
     act_ref,
     red_ref,
@@ -247,6 +258,7 @@
     for load in loads[1:]:
         load.wait()
 
+    x_ref[3 * HEAD :, :] = jnp.zeros((BLOCK, x_ref.shape[1]), BF16)
     def padded(ref, height, width_):
         pad_ref[...] = jnp.zeros_like(pad_ref)
         pad_ref[0:height, 0:width_] = ref[...]
@@ -279,7 +291,7 @@
 
     operator = (stiff, -m_e, -m_w, -m_n, -m_s)
     lf = columns(operator, 0)
-    lf_h[...], lf_l[...] = split(
+    lf_ref[...] = stacked(
         jnp.concatenate(
             [
                 lf[:ROWS],
@@ -290,7 +302,7 @@
         )
     )
     lg = columns(operator, TOP)
-    lg_h[...], lg_l[...] = split(
+    lg_ref[...] = stacked(
         jnp.concatenate(
             [
                 lg[:ROWS],
@@ -302,7 +314,7 @@
             axis=0,
         )
     )
-    s_h[...], s_l[...] = split(
+    s_ref[...] = stacked(
         jnp.concatenate(
             [stiff[:ROWS], cw[:FACES], cs[:FACES], pick[east][:FACES], pick[north][:FACES]], axis=0
         )
@@ -441,14 +453,11 @@
                 jnp.where(tall % TB == 0, unpack_y(y_in.at[1], q, 0), roll(v, 1)),
             )
             for i, part in enumerate(parts):
-                at = slice(i * BLOCK, (i + 1) * BLOCK)
-                x_h[at, span(q)], x_l[at, span(q)] = split(part)
-
-    def apply_block(l_h, l_l):
-        k = 5 * BLOCK
-        return (
-            dot(l_h[:, :k], x_h[...]) + dot(l_h[:, :k], x_l[...]) + dot(l_l[:, :k], x_h[...])
-        )
+                high, low = split(part)
+                at = i * BLOCK
+                x_ref[at : at + BLOCK, span(q)] = high
+                x_ref[at + HEAD : at + HEAD + BLOCK, span(q)] = low
+                x_ref[at + 2 * HEAD : at + 2 * HEAD + BLOCK, span(q)] = high
 
     def column(x):
         return jnp.sum(x, axis=0, keepdims=True)
@@ -470,21 +479,25 @@
         exchange(ar_ref.at[k], ar_ref.at[k], ar_send.at[k], ar_recv.at[k], True) for k in range(3)
     ]
 
-    def quadratic(b_ref, first, image_ref, alpha, base_ref, phase, slot):
+    def residual(b_ref, first, image_ref, alpha):
         for q in range(probes):
             a = alpha[q : q + 1, :]
-            image_ref[:, span(q)] = -a * image_ref[:, span(q)]
-            at = slice(first, first + BLOCK)
-            image_ref[at, span(q)] = image_ref[at, span(q)] + b_ref[:, span(q)]
-            r_h[:, span(q)], r_l[:, span(q)] = split(image_ref[:, span(q)])
-        sr_ref[...] = (
-            dot(s_h[:, :ROWS], r_h[...])
-            + dot(s_h[:, :ROWS], r_l[...])
-            + dot(s_l[:, :ROWS], r_h[...])
-        )
-        return edges(phase)
-
-    def quadratic_end(image_ref, alpha, base_ref, phase, slot):
+            r = -a * image_ref[:, span(q)]
+            last = first + BLOCK
+            parts = [r[first:last] + b_ref[:, span(q)], r[last:]]
+            r = jnp.concatenate(([r[:first]] if first else []) + parts, axis=0)
+            image_ref[:, span(q)] = r
+            high, low = split(r[:HEAD])
+            r_ref[0:HEAD, span(q)] = high
+            r_ref[HEAD : 2 * HEAD, span(q)] = low
+            r_ref[2 * HEAD : 3 * HEAD, span(q)] = high
+            end = r[HEAD:]
+            high = end.astype(BF16).astype(F32)
+            mixed = high + pltpu.roll(end - high, 1, 0) + pltpu.roll(high, 2, 0)
+            r_ref[3 * HEAD :, span(q)] = mixed.astype(BF16)
+        sr_ref[...] = dot(s_ref[...], r_ref[...])
+
+    def quadratic(image_ref, alpha, base_ref, phase, slot):
         face = lane_of(FACES)
         for q in range(probes):
             a = alpha[q : q + 1, :]
@@ -514,7 +527,7 @@
     f_start()
     f_receive()
     spread(f_ref, fx_in, fy_in)
-    got = apply_block(lf_h, lf_l)
+    got = dot(lf_ref[...], x_ref[...])
     u_ref[...] = got[:ROWS]
     gf_ref[...] = got[ROWS:]
     for q in range(probes):
@@ -543,7 +556,7 @@
 
     g_receive()
     spread(g_ref, gx_in, gy_in)
-    got = apply_block(lg_h, lg_l)
+    got = dot(lg_ref[...], x_ref[...])
     w_ref[...] = got[:ROWS]
     gg_ref[...] = got[ROWS : ROWS + 2 * FACES]
     sr_ref[0 : 2 * FACES, :] = got[ROWS + 2 * FACES :]
@@ -560,9 +573,9 @@
     reduces[0][1]()
     rr0, dad0 = from_slots(0, 2)
     alpha0 = rr0 / dad0
-    quadratic(f_ref, 0, u_ref, alpha0, gf_ref, 0, 0)
+    residual(f_ref, 0, u_ref, alpha0)
     u_receive()
-    quadratic_end(u_ref, alpha0, gf_ref, 0, 0)
+    quadratic(u_ref, alpha0, gf_ref, 0, 0)
 
     for q in range(probes):
         act_ref[q * BLOCK : (q + 1) * BLOCK, :] = scale * w_ref[0:BLOCK, span(q)]
@@ -577,11 +590,14 @@
     reduces[1][1]()
     qq0, ded0 = from_slots(1, 2)
     gamma0 = qq0 / ded0
-    quadratic(g_ref, TOP, w_ref, gamma0, gg_ref, 1, 2)
+    residual(g_ref, TOP, w_ref, gamma0)
     w_receive()
-    quadratic_end(w_ref, gamma0, gg_ref, 1, 2)
+    quadratic(w_ref, gamma0, gg_ref, 1, 2)
     to_slot(2, tuple(red_ref[k] for k in range(4)))
     reduces[2][0]()
+    for q in range(probes):
+        adj_ref[:, q, :] = w_ref[0:DOF, span(q)]
+        adjg_ref[:, q, :] = g_ref[0:BASAL, span(q)]
     reduces[2][1]()
     rr1, rar, qq1, qaq = from_slots(2, 4)
     beta = rr1 / rr0
@@ -593,11 +609,8 @@
     on_r = factor * gamma1
     on_w = -on_r * gamma0
 
-    for q in range(probes):
-        w_ref[:, span(q)] = on_r[q : q + 1, :] * w_ref[:, span(q)]
-        at = slice(TOP, TOP + BLOCK)
-        w_ref[at, span(q)] = w_ref[at, span(q)] + on_b[q : q + 1, :] * g_ref[:, span(q)]
-        adj_ref[:, q, :] = w_ref[0:DOF, span(q)]
+    adj_ref[0:TOP] = on_r[None] * adj_ref[0:TOP]
+    adj_ref[TOP:] = on_r[None] * adj_ref[TOP:] + on_b[None] * adjg_ref[...]
     out_finish()
     f_finish()
     g_finish()
@@ -648,22 +661,18 @@
         vm((BLOCK, LANES), F32),
         vm((BLOCK, LANES), F32),
         vm((BLOCK, LANES), F32),
-        vm((ROWS + 2 * FACES, LANES), BF16),
-        vm((ROWS + 2 * FACES, LANES), BF16),
-        vm((ROWS + 4 * FACES, LANES), BF16),
-        vm((ROWS + 4 * FACES, LANES), BF16),
-        vm((ROWS + 4 * FACES, LANES), BF16),
-        vm((ROWS + 4 * FACES, LANES), BF16),
+        vm((ROWS + 2 * FACES, DEPTH), BF16),
+        vm((ROWS + 4 * FACES, DEPTH), BF16),
+        vm((ROWS + 4 * FACES, DEPTH), BF16),
+        vm(probes.shape, F32),
         vm((BLOCK, full), F32),
         vm((BLOCK, full), F32),
         vm((ROWS, full), F32),
         vm((ROWS, full), F32),
         vm((2 * FACES, full), F32),
         vm((2 * FACES, full), F32),
-        vm((5 * BLOCK, full), BF16),
-        vm((5 * BLOCK, full), BF16),
-        vm((ROWS, full), BF16),
-        vm((ROWS, full), BF16),
+        vm((DEPTH, full), BF16),
+        vm((DEPTH, full), BF16),
         vm((ROWS + 4 * FACES, full), F32),
         vm((width, LANES), F32),
         vm((4, number, LANES), F32),

time: 32.7 us -> 30.9 us (0.945)
  Pallas kernels: 30.5 us -> 28.6 us
    pallas_call x1, Pallas kernels: 30.5 us -> 28.6 us  [local(): pl.pallas_call(functools.partial(kernel, count, number), out_shape=(jax.S...]
where the time goes in v4:
time: 30.9 us; the launch traced here: 30.7 us
  Pallas kernels  28.6 us (93%)
  local copies, waits for them, and re-layouts  1.47 us (5%)
  between operations  0.64 us (2%)
    pallas_call x1, Pallas kernels, local(): pl.pallas_call(functools.partial(kernel, count, number), out_shape=(jax.S...  28.6 us
    unnamed x2, local copies, waits for them, and re-layouts  1.47 us

profile of v4, /device:TPU:0, one launch (start us, length us, event | category | flops | bytes accessed | tf_op | source)
XLA Modules:
  0.0 30.7 jit_solution(12785255025845178525)
XLA Ops:
  0.6 28.6 %shard_map.104 = (f32[9,16,128]{2,1,0:T(8,128)S(1)}, f32[81,16,128]{2,1,0:T(8,128)S(1)}) custom-call(f32[81,128]{1,0:T(8,128)} %vel_hbm.1, f32[1,128]{1,0:T(1,128)} %bitcast.1, f32[9,128]{1,0:T(8,128)} %fric_hbm.1, f32[9,128]{1,0:T(8,128)} %obs_hbm.1, f32[81,81]{1,0:T(8,128)} %stiff_hbm.1, f32[27,27]{1,0:T(8,128)} %coup_hbm.1, s32[4,27]{1,0:T(4,128)} %faces_hbm.1, ...), custom_call_target="tpu_custom_call" | custom-call | tf_op jit(solution)/shard_map/pallas_call | solution.py:716
  29.3 0.6 %copy.13 = f32[9,16,128]{2,1,0:T(8,128)} copy(f32[9,16,128]{2,1,0:T(8,128)S(1)} %get-tuple-element.4) | data formatting | bytes 147456
  29.9 0.8 %copy.14 = f32[81,16,128]{2,1,0:T(8,128)} copy(f32[81,16,128]{2,1,0:T(8,128)S(1)} %get-tuple-element.5) | data formatting | bytes 1327104

commit v5 on v4

--- a/solution.py
+++ b/solution.py
@@ -519,12 +519,20 @@
 
     out_receive()
     arrived = recv1[...].reshape(count * share, width)
-    tile_probe = dot_exact(arrived, order, ((0,), (0,)))
+    high, low = split(arrived)
+    parts = jnp.concatenate([high, low], axis=0)
+    twice = jnp.concatenate([order, order], axis=0).astype(BF16)
+    tile_probe = lax.dot_general(
+        parts, twice, (((0,), (0,)), ((), ())), preferred_element_type=F32
+    )
     for q in range(probes):
         f_ref[:, span(q)] = -scale * tile_probe[q * BLOCK : (q + 1) * BLOCK]
     send_edges(f_ref, fx_out, fy_out)
     f_start, f_receive, f_finish = halo(fx_out, fy_out, fx_in, fy_in, 0)
     f_start()
+    for q in range(probes):
+        f = f_ref[:, span(q)]
+        red_ref[0, q : q + 1, :] = column(f * f)
     f_receive()
     spread(f_ref, fx_in, fy_in)
     got = dot(lf_ref[...], x_ref[...])
@@ -537,9 +545,7 @@
     g_start, g_receive, g_finish = halo(gx_out, gy_out, gx_in, gy_in, 1)
     g_start()
     for q in range(probes):
-        f = f_ref[:, span(q)]
-        red_ref[0, q : q + 1, :] = column(f * f)
-        red_ref[1, q : q + 1, :] = column(f * u_ref[0:BLOCK, span(q)])
+        red_ref[1, q : q + 1, :] = column(f_ref[:, span(q)] * u_ref[0:BLOCK, span(q)])
     to_slot(0, (red_ref[0], red_ref[1]))
     reduces[0][0]()
 
@@ -553,6 +559,9 @@
     cy_out[0] = compress(cs[:FACES, :ROWS], pack_y(read_u, ROWS, 0, probes))
     u_start, u_receive, u_finish = edges(0)
     u_start()
+    for q in range(probes):
+        g = g_ref[:, span(q)]
+        red_ref[2, q : q + 1, :] = column(g * g)
 
     g_receive()
     spread(g_ref, gx_in, gy_in)
@@ -560,16 +569,14 @@
     w_ref[...] = got[:ROWS]
     gg_ref[...] = got[ROWS : ROWS + 2 * FACES]
     sr_ref[0 : 2 * FACES, :] = got[ROWS + 2 * FACES :]
+    for q in range(probes):
+        red_ref[3, q : q + 1, :] = column(g_ref[:, span(q)] * w_ref[TOP : TOP + BLOCK, span(q)])
+    to_slot(1, (red_ref[2], red_ref[3]))
+    reduces[1][0]()
     cx_out[1] = pack_x(lambda q: sr_ref[0:FACES, span(q)], FACES, 0, probes)
     cy_out[1] = pack_y(lambda q: sr_ref[FACES : 2 * FACES, span(q)], FACES, 0, probes)
     w_start, w_receive, w_finish = edges(1)
     w_start()
-    for q in range(probes):
-        g = g_ref[:, span(q)]
-        red_ref[0, q : q + 1, :] = column(g * g)
-        red_ref[1, q : q + 1, :] = column(g * w_ref[TOP : TOP + BLOCK, span(q)])
-    to_slot(1, (red_ref[0], red_ref[1]))
-    reduces[1][0]()
     reduces[0][1]()
     rr0, dad0 = from_slots(0, 2)
     alpha0 = rr0 / dad0
@@ -579,7 +586,12 @@
 
     for q in range(probes):
         act_ref[q * BLOCK : (q + 1) * BLOCK, :] = scale * w_ref[0:BLOCK, span(q)]
-    placed = dot_exact(order, act_ref[...], ((1,), (1,)))
+    high, low = split(act_ref[...])
+    parts = jnp.concatenate([high, low], axis=1)
+    twice = jnp.concatenate([order, order], axis=1).astype(BF16)
+    placed = lax.dot_general(
+        twice, parts, (((1,), (1,)), ((), ())), preferred_element_type=F32
+    )
     send2[...] = placed.reshape(count, share, width)
     recv2[pl.ds(me, 1)] = send2[pl.ds(me, 1)]
     home_start, home_receive, home_finish = exchange(

time: 30.9 us -> 30.1 us (0.974)
  Pallas kernels: 28.6 us -> 27.9 us
    pallas_call x1, Pallas kernels: 28.6 us -> 27.9 us  [local(): pl.pallas_call(functools.partial(kernel, count, number), out_shape=(jax.S...]
where the time goes in v5:
time: 30.1 us; the launch traced here: 30 us
  Pallas kernels  27.9 us (93%)
  local copies, waits for them, and re-layouts  1.47 us (5%)
  between operations  0.64 us (2%)
    pallas_call x1, Pallas kernels, local(): pl.pallas_call(functools.partial(kernel, count, number), out_shape=(jax.S...  27.9 us
    unnamed x2, local copies, waits for them, and re-layouts  1.47 us

profile of v5, /device:TPU:0, one launch (start us, length us, event | category | flops | bytes accessed | tf_op | source)
XLA Modules:
  0.0 30.0 jit_solution(4129212040201388204)
XLA Ops:
  0.6 27.9 %shard_map.104 = (f32[9,16,128]{2,1,0:T(8,128)S(1)}, f32[81,16,128]{2,1,0:T(8,128)S(1)}) custom-call(f32[81,128]{1,0:T(8,128)} %vel_hbm.1, f32[1,128]{1,0:T(1,128)} %bitcast.1, f32[9,128]{1,0:T(8,128)} %fric_hbm.1, f32[9,128]{1,0:T(8,128)} %obs_hbm.1, f32[81,81]{1,0:T(8,128)} %stiff_hbm.1, f32[27,27]{1,0:T(8,128)} %coup_hbm.1, s32[4,27]{1,0:T(4,128)} %faces_hbm.1, ...), custom_call_target="tpu_custom_call" | custom-call | tf_op jit(solution)/shard_map/pallas_call | solution.py:728
  28.5 0.6 %copy.13 = f32[9,16,128]{2,1,0:T(8,128)} copy(f32[9,16,128]{2,1,0:T(8,128)S(1)} %get-tuple-element.4) | data formatting | bytes 147456
  29.1 0.8 %copy.14 = f32[81,16,128]{2,1,0:T(8,128)} copy(f32[81,16,128]{2,1,0:T(8,128)S(1)} %get-tuple-element.5) | data formatting | bytes 1327104

commit v6 on v5

--- a/solution.py
+++ b/solution.py
@@ -462,6 +462,9 @@
     def column(x):
         return jnp.sum(x, axis=0, keepdims=True)
 
+    def fold(x):
+        return jnp.sum(x.reshape(x.shape[0] // 8, 8, LANES), axis=0)
+
     def to_slot(which, values):
         out = jnp.zeros((probes, LANES), F32)
         for k, v in enumerate(values):
@@ -503,8 +506,8 @@
             a = alpha[q : q + 1, :]
             r = image_ref[:, span(q)]
             red_ref[slot, q : q + 1, :] = column(r * r)
-            t = column(visc * sr_ref[0:ROWS, span(q)] * r)
-            t += column(fric16 * r[0:BLOCK] * r[0:BLOCK])
+            t = visc * fold(sr_ref[0:ROWS, span(q)] * r)
+            t += fold(fric16 * r[0:BLOCK] * r[0:BLOCK])
             at = ROWS
             cwr = sr_ref[at : at + FACES, span(q)]
             csr = sr_ref[at + FACES : at + 2 * FACES, span(q)]
@@ -514,8 +517,8 @@
             hy = base_ref[FACES : 2 * FACES, span(q)] - a * unpack_y(cy_in.at[phase], q, TB - 1)
             nx = jnp.where(face // TB == 3, hx, roll(cwr, -TB))
             ny = jnp.where(face % TB == TB - 1, hy, roll(csr, -1))
-            t -= 2.0 * column(per * nx + pnr * ny)
-            red_ref[slot + 1, q : q + 1, :] = t
+            t -= 2.0 * fold(per * nx + pnr * ny)
+            red_ref[slot + 1, q : q + 1, :] = column(t)
 
     out_receive()
     arrived = recv1[...].reshape(count * share, width)

time: 30.1 us -> 30.1 us (level)
  no operation moved by 1% of the time
where the time goes in v6:
time: 30.1 us; the launch traced here: 29.9 us
  Pallas kernels  27.8 us (92%)
  local copies, waits for them, and re-layouts  1.47 us (5%)
  between operations  0.64 us (2%)
    pallas_call x1, Pallas kernels, local(): pl.pallas_call(functools.partial(kernel, count, number), out_shape=(jax.S...  27.8 us
    unnamed x2, local copies, waits for them, and re-layouts  1.47 us

profile of v6, /device:TPU:0, one launch (start us, length us, event | category | flops | bytes accessed | tf_op | source)
XLA Modules:
  0.0 29.9 jit_solution(11319148861389130605)
XLA Ops:
  0.6 27.8 %shard_map.104 = (f32[9,16,128]{2,1,0:T(8,128)S(1)}, f32[81,16,128]{2,1,0:T(8,128)S(1)}) custom-call(f32[81,128]{1,0:T(8,128)} %vel_hbm.1, f32[1,128]{1,0:T(1,128)} %bitcast.1, f32[9,128]{1,0:T(8,128)} %fric_hbm.1, f32[9,128]{1,0:T(8,128)} %obs_hbm.1, f32[81,81]{1,0:T(8,128)} %stiff_hbm.1, f32[27,27]{1,0:T(8,128)} %coup_hbm.1, s32[4,27]{1,0:T(4,128)} %faces_hbm.1, ...), custom_call_target="tpu_custom_call" | custom-call | tf_op jit(solution)/shard_map/pallas_call | solution.py:731
  28.5 0.6 %copy.13 = f32[9,16,128]{2,1,0:T(8,128)} copy(f32[9,16,128]{2,1,0:T(8,128)S(1)} %get-tuple-element.4) | data formatting | bytes 147456
  29.1 0.8 %copy.14 = f32[81,16,128]{2,1,0:T(8,128)} copy(f32[81,16,128]{2,1,0:T(8,128)S(1)} %get-tuple-element.5) | data formatting | bytes 1327104
